TPU v7x, 128 devices: a whole 4x4x4 slice. The times are simulated.
128 devices in a mesh: tm: 8 (over z, x_hi), space: 16 (over x_lo, y, core).
Axes of the slice: x: 4 (x_hi: 2, x_lo: 2; x = x_hi * 2 + x_lo), y: 4, z: 4, core: 2. Of those that a mesh axis runs over, the one named last changes fastest.
Arguments:
- solutions: bfloat16 [128, 64, 2, 3, 8192], P(('tm', 'space')), may hold values from -6 to 6
- eigvecs: bfloat16 [128, 128, 2, 3, 8192], P('tm', None, None, None, 'space'), may hold values from -0.02734375 to 0.02734375
Outputs:
- perambulator: float32 [128, 128, 128], P('tm', 'space')
All inputs are finite; a program needn't handle non-finite values.
Results may differ from a plain program's by a relative error of at most 0.0003.
Values may be sent and summed in bfloat16 or wider, within the bound.
No kernel may reach another device: no remote copies, remote signals or barrier semaphores. Data moves between devices by JAX's collectives and lax.ppermute only.
A program may use at most 192 MiB of HBM per device.

v0:
```python
import jax
import jax.numpy as jnp
from jax import lax
from jax.sharding import PartitionSpec as P


def project(vectors, fields):
    real_part = jnp.einsum("tnrcx,tmrcx->tnm", vectors, fields, preferred_element_type=jnp.float32)
    imag_part = jnp.einsum(
        "tncx,tmcx->tnm", vectors[:, :, 0], fields[:, :, 1], preferred_element_type=jnp.float32
    )
    imag_part = imag_part - jnp.einsum(
        "tncx,tmcx->tnm", vectors[:, :, 1], fields[:, :, 0], preferred_element_type=jnp.float32
    )
    return jnp.stack([real_part, imag_part], axis=2)


def body(solutions, eigvecs):
    partials = project(
        eigvecs, lax.all_to_all(solutions, "space", split_axis=4, concat_axis=0, tiled=True)
    )
    partials = partials.reshape(partials.shape[0], partials.shape[1], -1)
    summed = lax.psum(partials, "space")
    share_rows = summed.shape[1] // lax.axis_size("space")
    return lax.dynamic_slice_in_dim(summed, lax.axis_index("space") * share_rows, share_rows, 1)


def solution(mesh):
    placed = (P(("tm", "space"), None, None, None, None), P("tm", None, None, None, "space"))
    return jax.shard_map(
        body, mesh=mesh, in_specs=placed, out_specs=P("tm", "space", None), check_vma=False
    )
```

profile of v0, /device:TPU:1, one launch (start us, length us, event | category | flops | bytes accessed | tf_op | source)
XLA Modules:
  0.0 359.6 jit_solution(3566807861098760917)
XLA Ops:
  6.5 31.9 %copy.21 = bf16[1,64,2,3,8192]{1,2,3,0,4:T(2,128)(2,1)} copy(bf16[1,64,2,3,8192]{4,2,3,1,0:T(2,128)(2,1)} %param.2) | data formatting | bytes 12582912 | tf_op args[0]
  38.4 16.7 %reshape.7 = bf16[16,2,98304]{2,1,0:T(2,128)(2,1)} reshape(bf16[8192,1,3,2,64]{4,3,2,1,0:T(2,128)(2,1)} %bitcast.56) | data formatting | bytes 12582912
  55.1 6.9 %all-to-all-start = ((bf16[16,2,98304]{2,1,0:T(2,128)(2,1)}), bf16[16,2,98304]{2,1,0:T(2,128)(2,1)}, u32[]{:S(2)}, u32[]{:S(2)}) async-start(bf16[16,2,98304]{2,1,0:T(2,128)(2,1)} %reshape.7), calls=%async_computation | async-start | bytes 12582912 | tf_op jit(solution)/shard_map/all_to_all | solution.py:20
  62.1 0.0 all-reduce.2.cloned.1.call-start
  62.1 25.8 %fusion.12 = (bf16[16,128,1,3,512]{4,2,3,1,0:T(2,128)(2,1)}, bf16[16,128,1,3,512]{4,2,3,1,0:T(2,128)(2,1)}) fusion(bf16[16,128,2,3,512]{4,2,3,1,0:T(2,128)(2,1)} %param.3), kind=kLoop, calls=%fused_computation.16 | loop fusion | bytes 25165824 | tf_op jit(solution)/shard_map/slice | solution.py:13
  87.9 62.7 %all-to-all-done = bf16[16,2,98304]{2,1,0:T(2,128)(2,1)} async-done(((bf16[16,2,98304]{2,1,0:T(2,128)(2,1)}), bf16[16,2,98304]{2,1,0:T(2,128)(2,1)}, u32[]{:S(2)}, u32[]{:S(2)}) %all-to-all-start) | async-done | bytes 6291488 | tf_op jit(solution)/shard_map/all_to_all | solution.py:20
  150.6 16.4 %reshape.8 = bf16[8192,1,3,2,64]{4,3,2,1,0:T(2,128)(2,1)} reshape(bf16[16,2,98304]{2,1,0:T(2,128)(2,1)} %all-to-all-done) | data formatting | bytes 12582912
  167.0 29.4 %copy.23 = bf16[1,64,2,3,16,512]{5,1,2,3,4,0:T(8,128)(2,1)} copy(bf16[1,64,2,3,16,512]{1,2,3,5,4,0:T(2,128)(2,1)} %bitcast.55) | data formatting | bytes 12582912 | tf_op jit(solution)/shard_map/all_to_all | solution.py:20
  196.5 10.8 %fusion.6 = f32[16,128,1,64]{1,3,0,2:T(8,128)S(1)} fusion(bf16[16,128,2,3,512]{4,2,3,1,0:T(2,128)(2,1)} %param.3, bf16[1,64,2,3,16,512]{5,1,2,3,4,0:T(8,128)(2,1)} %copy.23), kind=kOutput, calls=%fused_computation.10 | convolution fusion | flops 805306368 | bytes 19398656 | tf_op jit(solution)/shard_map/tnrcx,tmrcx->tnm/dot_general | solution.py:8
  207.3 0.0 copy-start
  207.3 7.9 %fusion.4 = f32[16,128,64]{1,2,0:T(8,128)S(1)} fusion(bf16[16,64,2,3,512]{4,1,2,3,0:T(8,128)(2,1)} %bitcast.57, bf16[16,128,1,3,512]{4,2,3,1,0:T(2,128)(2,1)} %get-tuple-element.6), kind=kOutput, calls=%fused_computation.8 | convolution fusion | flops 402653184 | bytes 16252928 | tf_op jit(solution)/shard_map/tncx,tmcx->tnm/dot_general | solution.py:9
  215.2 0.0 copy-done
  215.2 6.9 %fusion.10 = f32[16,128,1,64]{1,3,0,2:T(8,128)S(1)} fusion(f32[16,128,64]{1,2,0:T(8,128)S(1)} %fusion.4, bf16[16,64,2,3,512]{4,1,2,3,0:T(8,128)(2,1)S(1)} %bitcast.58, bf16[16,128,1,3,512]{4,2,3,1,0:T(2,128)(2,1)} %get-tuple-element.5), kind=kOutput, calls=%fused_computation.12 | convolution fusion | flops 402784256 | bytes 10485760 | tf_op jit(solution)/shard_map/tncx,tmcx->tnm/dot_general | solution.py:12
  222.1 0.1 pad_maximum_fusion
  222.2 1.1 copy.27
  223.3 0.0 all-reduce.2.cloned.1.call-update
  223.3 127.0 %all-reduce.2.cloned.1.call-done = f32[16,128,128]{1,2,0:T(8,128)} async-done(((f32[16,128,128]{1,2,0:T(8,128)}), f32[16,128,128]{1,2,0:T(8,128)}) %all-reduce.2.cloned.1.call-update) | async-done | bytes 1048592 | tf_op jit(solution)/shard_map/psum | solution.py:23
  350.3 1.6 constant_dynamic-slice_fusion
  351.9 0.9 copy.28
Async XLA Ops:
  55.1 95.5 %all-to-all-start = ((bf16[16,2,98304]{2,1,0:T(2,128)(2,1)}), bf16[16,2,98304]{2,1,0:T(2,128)(2,1)}, u32[]{:S(2)}, u32[]{:S(2)}) async-start(bf16[16,2,98304]{2,1,0:T(2,128)(2,1)} %reshape.7), calls=%async_computation | async-start | bytes 12582912 | tf_op jit(solution)/shard_map/all_to_all | solution.py:20
  62.1 288.2 %all-reduce.2.cloned.1.call-start = ((), (), s32[]{:S(2)}) async-start(), calls=%async_computation.1 | async-start | bytes 2097152 | tf_op jit(solution)/shard_map/psum | solution.py:23
  207.3 7.9 %copy-start = (bf16[1,64,2,3,16,512]{5,1,2,3,4,0:T(8,128)(2,1)S(1)}, bf16[1,64,2,3,16,512]{5,1,2,3,4,0:T(8,128)(2,1)}, u32[]{:S(2)}) copy-start(bf16[1,64,2,3,16,512]{5,1,2,3,4,0:T(8,128)(2,1)} %copy.23) | copy-start | bytes 18874372
Sparse Core Ops, SparseCore 0:
  223.4 126.8 all-reduce.1
where the time goes:
time: 362 us; the launch traced here: 360 us
  waiting for transfers between devices  190 us (52%)
  local copies, waits for them, and re-layouts  124 us (34%)
  matrix products  25.6 us (7%)
  between operations  13.5 us (4%)
  starting transfers between devices  6.95 us (2%)
    psum x1, waiting for transfers between devices, body(): summed = lax.psum(partials, 'space')  127 us
    unnamed x5, local copies, waits for them, and re-layouts  65 us
    all_to_all x1, waiting for transfers between devices, body(): lax.all_to_all(solutions, 'space', split_axis=4, concat_axis=0, tiled=True)  62.7 us
    all_to_all x1, local copies, waits for them, and re-layouts, body(): lax.all_to_all(solutions, 'space', split_axis=4, concat_axis=0, tiled=True)  29.4 us
    slice x1, local copies, waits for them, and re-layouts, project(): vectors[:, :, 1]  25.8 us
    dot_general x1, matrix products, project(): jnp.einsum('tnrcx,tmrcx->tnm', vectors, fields, preferred_element_type=jn...  10.8 us
    dot_general x1, matrix products, project(): jnp.einsum('tncx,tmcx->tnm', vectors[:, :, 0], fields[:, :, 1], preferred...  7.9 us
  transfers between devices with their start and end apart: 2, of which 2 were waited for; matrix products, arithmetic and copies ran while one was open for 7% of the time, Pallas kernels for 0%

commit v1 on v0

v1 whole, which is shorter than its diff:
```python
import jax
import jax.numpy as jnp
from jax import lax
from jax.experimental import pallas as pl
from jax.experimental.pallas import tpu as pltpu
from jax.sharding import PartitionSpec as P

LANES = 128


def tile_view(a, groups):
    outer, rows, parts, colors, sites = a.shape
    a = a.reshape(outer, rows, parts, colors, groups, sites // groups // LANES, LANES)
    a = a.transpose(0, 1, 3, 4, 5, 2, 6)
    return a.reshape(outer, rows, colors, groups, -1, LANES)


def unpack_kernel(src, dst, wide):
    _, rows, colors, groups, inner, _ = src.shape
    stride = colors * groups * inner
    wide[...] = src[...].astype(jnp.float32).reshape(wide.shape)
    for g in range(groups):
        for c in range(colors):
            for k in range(inner):
                lines = wide[pl.ds((c * groups + g) * inner + k, rows, stride=stride), :]
                lane = (c * (inner // 2) + k // 2) * LANES
                dst[g, k % 2, :, pl.ds(lane, LANES)] = lines.astype(jnp.bfloat16)


def unpack(view, block_rows):
    outer, rows, colors, groups, inner, _ = view.shape
    depth = colors * inner // 2 * LANES
    return pl.pallas_call(
        unpack_kernel,
        grid=(outer, rows // block_rows),
        in_specs=[
            pl.BlockSpec((1, block_rows, colors, groups, inner, LANES), lambda a, b: (a, b, 0, 0, 0, 0))
        ],
        out_specs=pl.BlockSpec((groups, 2, block_rows, depth), lambda a, b: (a, 0, b, 0)),
        out_shape=jax.ShapeDtypeStruct((outer * groups, 2, rows, depth), view.dtype),
        scratch_shapes=[pltpu.VMEM((block_rows * colors * groups * inner, LANES), jnp.float32)],
        compiler_params=pltpu.CompilerParams(vmem_limit_bytes=40 * 2**20),
        cost_estimate=pl.CostEstimate(flops=0, bytes_accessed=4 * view.size, transcendentals=0),
    )(view)


def product_kernel(vec, sol, out):
    rows = vec.shape[2]
    cols = sol.shape[2]
    e = vec[0].reshape(2 * rows, vec.shape[3])
    s = sol[0].reshape(2 * cols, sol.shape[3])
    g = lax.dot_general(e, s, (((1,), (1,)), ((), ())), preferred_element_type=jnp.float32)
    crossed = pltpu.roll(g[rows:], cols, 1)
    lane = lax.broadcasted_iota(jnp.int32, crossed.shape, 1)
    res = g[:rows] + jnp.where(lane < cols, crossed, -crossed)
    out[...] = res.reshape(out.shape)


def product(vec, sol, shares):
    times, _, rows, depth = vec.shape
    cols = sol.shape[2]
    return pl.pallas_call(
        product_kernel,
        grid=(times,),
        in_specs=[
            pl.BlockSpec((1, 2, rows, depth), lambda t: (t, 0, 0, 0)),
            pl.BlockSpec((1, 2, cols, depth), lambda t: (t, 0, 0, 0)),
        ],
        out_specs=pl.BlockSpec((shares, 1, rows // shares, 2 * cols), lambda t: (0, t, 0, 0)),
        out_shape=jax.ShapeDtypeStruct((shares, times, rows // shares, 2 * cols), jnp.float32),
        compiler_params=pltpu.CompilerParams(vmem_limit_bytes=40 * 2**20),
        cost_estimate=pl.CostEstimate(
            flops=8 * times * rows * cols * depth, bytes_accessed=2 * (vec.size + sol.size), transcendentals=0
        ),
    )(vec, sol)


def body(solutions, eigvecs):
    shares = lax.axis_size("space")
    sol = unpack(tile_view(solutions, shares), 16)
    sol = lax.all_to_all(sol, "space", split_axis=0, concat_axis=0, tiled=True)
    vec = unpack(tile_view(eigvecs, 1), eigvecs.shape[1])
    partial = product(vec, sol, shares)
    partial = lax.all_to_all(partial, "space", split_axis=0, concat_axis=0, tiled=True)
    return jnp.sum(partial, axis=0)


def solution(mesh):
    placed = (P(("tm", "space"), None, None, None, None), P("tm", None, None, None, "space"))
    return jax.shard_map(
        body, mesh=mesh, in_specs=placed, out_specs=P("tm", "space", None), check_vma=False
    )
```

time: 362 us -> 152 us (0.42)
  waiting for transfers between devices: 190 us -> 70.8 us
  local copies, waits for them, and re-layouts: 124 us -> 9.92 us
  Pallas kernels: 0 us -> 36.2 us
  blocking collectives: 0 us -> 27 us
  matrix products: 25.6 us -> 0 us
  between operations: 13.5 us -> 0.04 us
    psum x1 -> x0, waiting for transfers between devices: 127 us -> none  [body(): summed = lax.psum(partials, 'space')]
    unnamed x5 -> x6, local copies, waits for them, and re-layouts: 65 us -> 9.92 us
    pallas_call x0 -> x3, Pallas kernels: none -> 36.2 us  [the longest x2 21.7 us: unpack(): pl.pallas_call(unpack_kernel, grid=(outer, rows // block_rows), in_specs=...]
    all_to_all x1 -> x0, local copies, waits for them, and re-layouts: 29.4 us -> none  [body(): lax.all_to_all(solutions, 'space', split_axis=4, concat_axis=0, tiled=True)]
    all_to_all x0 -> x1, blocking collectives: none -> 27 us  [body(): lax.all_to_all(partial, 'space', split_axis=0, concat_axis=0, tiled=True)]
    slice x1 -> x0, local copies, waits for them, and re-layouts: 25.8 us -> none  [project(): vectors[:, :, 1]]
    dot_general x3 -> x0, matrix products: 25.6 us -> none  [the longest x1 10.8 us: project(): jnp.einsum('tnrcx,tmrcx->tnm', vectors, fields, preferred_element_type=jn...]
    all_to_all x1, waiting for transfers between devices: 62.7 us -> 70.8 us  [body(): sol = lax.all_to_all(sol, 'space', split_axis=0, concat_axis=0, tiled=True)]
  transfers between devices with their start and end apart: 2 -> 1, of which waited for: 2 -> 1; matrix products, arithmetic and copies ran while one was open for 7% -> 0% of each run, Pallas kernels for 0% -> 9%
where the time goes in v1:
time: 152 us
  waiting for transfers between devices  70.8 us (47%)
  Pallas kernels  36.2 us (24%)
  blocking collectives  27 us (18%)
  local copies, waits for them, and re-layouts  9.92 us (7%)
  starting transfers between devices  6.91 us (5%)
    all_to_all x1, waiting for transfers between devices, body(): sol = lax.all_to_all(sol, 'space', split_axis=0, concat_axis=0, tiled=True)  70.8 us
    all_to_all x1, blocking collectives, body(): lax.all_to_all(partial, 'space', split_axis=0, concat_axis=0, tiled=True)  27 us
    pallas_call x2, Pallas kernels, unpack(): pl.pallas_call(unpack_kernel, grid=(outer, rows // block_rows), in_specs=...  21.7 us
    pallas_call x1, Pallas kernels, product(): pl.pallas_call(product_kernel, grid=(times,), in_specs=[pl.BlockSpec((1,...  14.5 us
    unnamed x6, local copies, waits for them, and re-layouts  9.92 us
    all_to_all x1, starting transfers between devices, body(): sol = lax.all_to_all(sol, 'space', split_axis=0, concat_axis=0, tiled=True)  6.91 us
  transfers between devices with their start and end apart: 1, of which 1 were waited for; matrix products, arithmetic and copies ran while one was open for 0% of the time, Pallas kernels for 9%

profile of v1, /device:TPU:1, one launch (start us, length us, event | category | flops | bytes accessed | tf_op | source)
XLA Modules:
  0.0 151.5 jit_solution(16568787495832529120)
XLA Ops:
  0.0 0.0 copy-start.2
  0.0 2.8 %copy-done.2 = bf16[1,64,2,3,8192]{4,2,3,1,0:T(2,128)(2,1)S(1)} copy-done((bf16[1,64,2,3,8192]{4,2,3,1,0:T(2,128)(2,1)S(1)}, bf16[1,64,2,3,8192]{4,2,3,1,0:T(2,128)(2,1)}, u32[]{:S(2)}) %copy-start.2) | copy-done | bytes 6291480
  2.8 8.5 %shard_map.29 = bf16[16,2,64,1536]{3,2,1,0:T(8,128)(2,1)S(1)} custom-call(bf16[1,64,3,16,8,128]{5,4,3,2,1,0:T(8,128)(2,1)S(1)} %bitcast.10), custom_call_target="tpu_custom_call" | custom-call | bytes 12582912 | tf_op jit(solution)/shard_map/pallas_call | solution.py:33
  11.3 0.0 copy-start.1
  11.3 2.6 %copy-done.1 = bf16[16,2,64,1536]{3,2,1,0:T(8,128)(2,1)} copy-done((bf16[16,2,64,1536]{3,2,1,0:T(8,128)(2,1)}, bf16[16,2,64,1536]{3,2,1,0:T(8,128)(2,1)S(1)}, u32[]{:S(2)}) %copy-start.1) | copy-done | bytes 6291480
  13.9 6.9 %all-to-all-start = ((bf16[16,2,64,1536]{3,2,1,0:T(8,128)(2,1)}), bf16[16,2,64,1536]{3,2,1,0:T(8,128)(2,1)}, u32[]{:S(2)}, u32[]{:S(2)}) async-start(bf16[16,2,64,1536]{3,2,1,0:T(8,128)(2,1)} %copy-done.1), calls=%async_computation | async-start | bytes 12582912 | tf_op jit(solution)/shard_map/all_to_all | solution.py:81
  20.8 13.2 %shard_map.28.vec = bf16[16,2,128,1536]{3,2,1,0:T(8,128)(2,1)S(1)} custom-call(bf16[16,128,3,1,8,128]{5,4,3,2,1,0:T(8,128)(2,1)} %bitcast.11), custom_call_target="tpu_custom_call" | custom-call | bytes 25165824 | tf_op jit(solution)/shard_map/pallas_call | solution.py:33
  34.0 0.0 copy-start
  34.0 4.5 %copy-done = bf16[16,2,128,1536]{3,2,1,0:T(8,128)(2,1)} copy-done((bf16[16,2,128,1536]{3,2,1,0:T(8,128)(2,1)}, bf16[16,2,128,1536]{3,2,1,0:T(8,128)(2,1)S(1)}, u32[]{:S(2)}) %copy-start) | copy-done | bytes 12582936
  38.5 70.8 %all-to-all-done.sol = bf16[16,2,64,1536]{3,2,1,0:T(8,128)(2,1)} async-done(((bf16[16,2,64,1536]{3,2,1,0:T(8,128)(2,1)}), bf16[16,2,64,1536]{3,2,1,0:T(8,128)(2,1)}, u32[]{:S(2)}, u32[]{:S(2)}) %all-to-all-start) | async-done | bytes 6291488 | tf_op jit(solution)/shard_map/all_to_all | solution.py:81
  109.4 14.5 %shard_map.30 = f32[16,16,8,128]{3,2,1,0:T(8,128)S(1)} custom-call(bf16[16,2,128,1536]{3,2,1,0:T(8,128)(2,1)} %copy-done, bf16[16,2,64,1536]{3,2,1,0:T(8,128)(2,1)} %all-to-all-done.sol), custom_call_target="tpu_custom_call" | custom-call | flops 1610612736 | bytes 18874368 | tf_op jit(solution)/shard_map/pallas_call | solution.py:62
  123.9 27.0 %all_to_all.10 = f32[16,16,8,128]{3,2,1,0:T(8,128)S(1)} all-to-all(f32[16,16,8,128]{3,2,1,0:T(8,128)S(1)} %shard_map.30), channel_id=1, replica_groups=mesh['tm'=8,'space'=16] {'space'}, dimensions={0} | all-to-all | bytes 2097152 | tf_op jit(solution)/shard_map/all_to_all | solution.py:84
  150.9 0.7 reduce_sum.9
Async XLA Ops:
  0.0 2.8 %copy-start.2 = (bf16[1,64,2,3,8192]{4,2,3,1,0:T(2,128)(2,1)S(1)}, bf16[1,64,2,3,8192]{4,2,3,1,0:T(2,128)(2,1)}, u32[]{:S(2)}) copy-start(bf16[1,64,2,3,8192]{4,2,3,1,0:T(2,128)(2,1)} %param.2) | copy-start | bytes 18874372
  11.3 2.6 %copy-start.1 = (bf16[16,2,64,1536]{3,2,1,0:T(8,128)(2,1)}, bf16[16,2,64,1536]{3,2,1,0:T(8,128)(2,1)S(1)}, u32[]{:S(2)}) copy-start(bf16[16,2,64,1536]{3,2,1,0:T(8,128)(2,1)S(1)} %shard_map.29) | copy-start | bytes 18874372
  13.9 95.5 %all-to-all-start = ((bf16[16,2,64,1536]{3,2,1,0:T(8,128)(2,1)}), bf16[16,2,64,1536]{3,2,1,0:T(8,128)(2,1)}, u32[]{:S(2)}, u32[]{:S(2)}) async-start(bf16[16,2,64,1536]{3,2,1,0:T(8,128)(2,1)} %copy-done.1), calls=%async_computation | async-start | bytes 12582912 | tf_op jit(solution)/shard_map/all_to_all | solution.py:81
  34.0 4.6 %copy-start = (bf16[16,2,128,1536]{3,2,1,0:T(8,128)(2,1)}, bf16[16,2,128,1536]{3,2,1,0:T(8,128)(2,1)S(1)}, u32[]{:S(2)}) copy-start(bf16[16,2,128,1536]{3,2,1,0:T(8,128)(2,1)S(1)} %shard_map.28.vec) | copy-start | bytes 37748740

commit v2 on v0

v2 whole, which is shorter than its diff:
```python
import jax
import jax.numpy as jnp
from jax import lax
from jax.experimental import pallas as pl
from jax.experimental.pallas import tpu as pltpu
from jax.sharding import PartitionSpec as P

LANES = 128
VMEM = 16 * 2**20
PACK_VMEM = 52 * 2**20
FREE = pl.CostEstimate(flops=0, bytes_accessed=0, transcendentals=0)
RING = 4
MOVES = [(1, 0), (0, 2), (1, 1), (1, 3), (0, 3), (0, 1), (1, 2)]


def tile_view(a, groups):
    outer, rows, parts, colors, sites = a.shape
    a = a.reshape(outer, rows, parts, colors, groups, sites // groups // LANES, LANES)
    a = a.transpose(0, 1, 3, 4, 5, 2, 6)
    return a.reshape(outer, rows, colors, groups, -1, LANES)


def split_lines(src, dst, wide, flip):
    _, rows, colors, groups, inner, _ = src.shape
    lines = colors * groups * inner
    stride = wide.shape[0] // rows
    for i in range(rows):
        wide[i * stride : i * stride + lines] = src[0, i].astype(jnp.float32).reshape(lines, LANES)
    for g in range(groups):
        for c in range(colors):
            for k in range(inner):
                picked = wide[pl.ds((c * groups + g) * inner + k, rows, stride=stride), :]
                lane = (c * (inner // 2) + k // 2) * LANES
                dst[g ^ flip, k % 2, :, pl.ds(lane, LANES)] = picked.astype(jnp.bfloat16)


def pack_solutions(view, where, block_rows=32):
    _, rows, colors, groups, inner, _ = view.shape
    count = where.shape[0] - 1
    depth = colors * inner // 2 * LANES

    def kernel(where, *refs):
        for n in range(count):
            split_lines(refs[n], refs[count + n], refs[2 * count], where[count])

    def source(n):
        return pl.BlockSpec(
            (1, block_rows, colors, 2, inner, LANES), lambda b, where: (0, b, 0, where[n], 0, 0)
        )

    return pl.pallas_call(
        kernel,
        grid_spec=pltpu.PrefetchScalarGridSpec(
            num_scalar_prefetch=1,
            grid=(rows // block_rows,),
            in_specs=[source(n) for n in range(count)],
            out_specs=[pl.BlockSpec((2, 2, block_rows, depth), lambda b, where: (0, 0, b, 0))] * count,
            scratch_shapes=[pltpu.VMEM((block_rows * (colors * 2 * inner + 8), LANES), jnp.float32)],
        ),
        out_shape=[jax.ShapeDtypeStruct((2, 2, rows, depth), view.dtype)] * count,
        compiler_params=pltpu.CompilerParams(vmem_limit_bytes=PACK_VMEM),
        cost_estimate=FREE,
    )(where, *[view] * count)


def pack_vectors(view, where):
    times, rows, colors, _, inner, _ = view.shape
    depth = colors * inner // 2 * LANES

    def kernel(where, src, dst, wide):
        split_lines(src, dst, wide, 0)

    return pl.pallas_call(
        kernel,
        grid_spec=pltpu.PrefetchScalarGridSpec(
            num_scalar_prefetch=1,
            grid=(times // 2,),
            in_specs=[
                pl.BlockSpec(
                    (1, rows, colors, 1, inner, LANES), lambda t, where: (2 * t + where[0], 0, 0, 0, 0, 0)
                )
            ],
            out_specs=pl.BlockSpec((1, 2, rows, depth), lambda t, where: (t, 0, 0, 0)),
            scratch_shapes=[pltpu.VMEM((rows * colors * inner, LANES), jnp.float32)],
        ),
        out_shape=jax.ShapeDtypeStruct((times // 2, 2, rows, depth), view.dtype),
        compiler_params=pltpu.CompilerParams(vmem_limit_bytes=PACK_VMEM),
        cost_estimate=FREE,
    )(where, view)


def product(near, far, sols, where, partial, shares):
    times, _, rows, depth = near.shape
    count = len(sols)
    cols = sols[0].shape[2]
    held = [] if partial is None else [partial]

    def kernel(where, near, far, *refs):
        out = refs[-1]

        def one(sol):
            g = jnp.zeros((2 * rows, 2 * cols), jnp.float32)
            for h, vec in enumerate((near, far)):
                g += lax.dot_general(
                    vec[0].reshape(2 * rows, depth),
                    sol[h].reshape(2 * cols, depth),
                    (((1,), (1,)), ((), ())),
                    preferred_element_type=jnp.float32,
                )
            crossed = pltpu.roll(g[rows:], cols, 1)
            lane = lax.broadcasted_iota(jnp.int32, crossed.shape, 1)
            out[...] = (g[:rows] + jnp.where(lane < cols, crossed, -crossed)).reshape(out.shape)

        for n in range(count):
            pl.when(pl.program_id(0) == n)(lambda n=n: one(refs[n]))

    vec_spec = pl.BlockSpec((1, 2, rows, depth), lambda i, where: (where[i], 0, 0, 0))
    sol_spec = pl.BlockSpec(sols[0].shape, lambda i, where: (0, 0, 0, 0))
    return pl.pallas_call(
        kernel,
        grid_spec=pltpu.PrefetchScalarGridSpec(
            num_scalar_prefetch=1,
            grid=(count,),
            in_specs=[vec_spec, vec_spec] + [sol_spec] * count + [pl.BlockSpec(memory_space=pl.ANY)] * len(held),
            out_specs=pl.BlockSpec(
                (shares, 1, rows // shares, 2 * cols), lambda i, where: (0, where[i], 0, 0)
            ),
        ),
        out_shape=jax.ShapeDtypeStruct((shares, times, rows // shares, 2 * cols), jnp.float32),
        input_output_aliases={3 + count: 0} if held else {},
        compiler_params=pltpu.CompilerParams(vmem_limit_bytes=VMEM),
        cost_estimate=FREE,
    )(where, near, far, *sols, *held)


def body(solutions, eigvecs):
    shares = lax.axis_size("space")
    chips = shares // 2
    me = lax.axis_index("space")
    core = me % 2
    x, y = me // 2 // RING, me // 2 % RING

    def route(dx, dy, dc):
        return [
            (i, (((i // 2 // RING) ^ dx) * RING + (i // 2 + dy) % RING) * 2 + (i % 2 ^ dc))
            for i in range(shares)
        ]

    def chip_at(dx, dy):
        return (x ^ dx) * RING + (y + dy) % RING

    def after(where, done):
        return lax.optimization_barrier((jnp.stack(where), done))[0]

    view = tile_view(solutions, shares)
    vectors = tile_view(eigvecs, 1)
    sends = {}

    def pack(moves, done):
        chunks = pack_solutions(view, after([chip_at(*m) for m in moves] + [core], done))
        sends.update(zip(moves, chunks))
        return chunks[-1]

    def send(moves):
        return {m: lax.ppermute(sends[m], "space", route(*m, 0)) for m in moves}

    done = core
    for moves in (MOVES[:1], MOVES[1:2], MOVES[2:4], MOVES[4:] + [(0, 0)]):
        done = pack(moves, done)
    arrived = send(MOVES)
    arrived[0, 0] = sends[0, 0]
    swapped = lax.ppermute(eigvecs, "space", route(0, 0, 1))
    where = after([core], done)
    near = pack_vectors(vectors, where)
    far = pack_vectors(tile_view(swapped, 1), where)
    partial = None
    for moves in ([(0, 0)], MOVES[:1], MOVES[1:2], MOVES[2:3], MOVES[3:4], MOVES[4:]):
        where = jnp.stack([chip_at(dx, -dy) for dx, dy in moves])
        partial = product(near, far, [arrived[m] for m in moves], where, partial, shares)
    partial = lax.all_to_all(partial, "space", split_axis=0, concat_axis=0, tiled=True)
    partial = partial.reshape(chips, 2, chips, -1, partial.shape[-1])
    total = jnp.sum(partial, axis=0)
    return jnp.swapaxes(total, 0, 1).reshape(shares, -1, total.shape[-1])


def solution(mesh):
    placed = (P(("tm", "space"), None, None, None, None), P("tm", None, None, None, "space"))
    return jax.shard_map(
        body, mesh=mesh, in_specs=placed, out_specs=P("tm", "space", None), check_vma=False
    )
```

time: 362 us -> 100 us (0.28)
  waiting for transfers between devices: 190 us -> 24.8 us
  local copies, waits for them, and re-layouts: 124 us -> 4.87 us
  Pallas kernels: 0 us -> 39.4 us
  matrix products: 25.6 us -> 0 us
  blocking collectives: 0 us -> 15 us
  between operations: 13.5 us -> 0.1 us
  starting transfers between devices: 6.95 us -> 15.2 us
    psum x1 -> x0, waiting for transfers between devices: 127 us -> none  [body(): summed = lax.psum(partials, 'space')]
    all_to_all x1 -> x0, waiting for transfers between devices: 62.7 us -> none  [body(): lax.all_to_all(solutions, 'space', split_axis=4, concat_axis=0, tiled=True)]
    unnamed x5 -> x10, local copies, waits for them, and re-layouts: 65 us -> 4.15 us
    pallas_call x0 -> x12, Pallas kernels: none -> 39.4 us  [the longest x2 19 us: pack_vectors(): pl.pallas_call(kernel, grid_spec=pltpu.PrefetchScalarGridSpec(num_scalar_...]
    all_to_all x1 -> x0, local copies, waits for them, and re-layouts: 29.4 us -> none  [body(): lax.all_to_all(solutions, 'space', split_axis=4, concat_axis=0, tiled=True)]
    slice x1 -> x0, local copies, waits for them, and re-layouts: 25.8 us -> none  [project(): vectors[:, :, 1]]
    dot_general x3 -> x0, matrix products: 25.6 us -> none  [the longest x1 10.8 us: project(): jnp.einsum('tnrcx,tmrcx->tnm', vectors, fields, preferred_element_type=jn...]
    ppermute x0 -> x8, waiting for transfers between devices: none -> 24.8 us  [the longest x7 24.8 us: send(): return {m: lax.ppermute(sends[m], 'space', route(*m, 0)) for m in moves}]
  transfers between devices with their start and end apart: 2 -> 8, of which waited for: 2 -> 4; matrix products, arithmetic and copies ran while one was open for 7% -> 0% of each run, Pallas kernels for 0% -> 37%
where the time goes in v2:
time: 100 us; the launch traced here: 99.7 us
  Pallas kernels  39.4 us (39%)
  waiting for transfers between devices  24.8 us (25%)
  starting transfers between devices  15.2 us (15%)
  blocking collectives  15 us (15%)
  local copies, waits for them, and re-layouts  4.87 us (5%)
    ppermute x7, waiting for transfers between devices, send(): return {m: lax.ppermute(sends[m], 'space', route(*m, 0)) for m in moves}  24.8 us
    pallas_call x2, Pallas kernels, pack_vectors(): pl.pallas_call(kernel, grid_spec=pltpu.PrefetchScalarGridSpec(num_scalar_...  19 us
    all_to_all x1, blocking collectives, body(): lax.all_to_all(partial, 'space', split_axis=0, concat_axis=0, tiled=True)  15 us
    ppermute x7, starting transfers between devices, send(): return {m: lax.ppermute(sends[m], 'space', route(*m, 0)) for m in moves}  13.8 us
    pallas_call x4, Pallas kernels, pack_solutions(): pl.pallas_call(kernel, grid_spec=pltpu.PrefetchScalarGridSpec(num_scalar_...  12.3 us
    pallas_call x6, Pallas kernels, product(): pl.pallas_call(kernel, grid_spec=pltpu.PrefetchScalarGridSpec(num_scalar_...  8.07 us
    unnamed x10, local copies, waits for them, and re-layouts  4.15 us
  transfers between devices with their start and end apart: 8, of which 4 were waited for; matrix products, arithmetic and copies ran while one was open for 0% of the time, Pallas kernels for 37%

profile of v2, /device:TPU:1, one launch (start us, length us, event | category | flops | bytes accessed | tf_op | source)
XLA Modules:
  0.0 99.7 jit_solution(7866024033914135140)
XLA Ops:
  0.0 1.4 %collective-permute-start = (bf16[16,128,2,3,512]{4,2,3,1,0:T(2,128)(2,1)}, bf16[16,128,2,3,512]{4,2,3,1,0:T(2,128)(2,1)}, u32[]{:S(2)}, u32[]{:S(2)}) collective-permute-start(bf16[16,128,2,3,512]{4,2,3,1,0:T(2,128)(2,1)} %param.3), channel_id=1, source_target_pairs={{0,1},{1,0},{2,3},{3,2},{4,5},{5,4},{6,7},{7,6},{8,9},{9,8},{10,11... | collective-permute-start | bytes 37748744 | tf_op jit(solution)/shard_map/ppermute | solution.py:172
  1.4 0.1 pad_add_fusion.2
  1.5 2.1 %shard_map.28 = bf16[2,2,64,1536]{3,2,1,0:T(8,128)(2,1)S(1)} custom-call(s32[2]{0:T(128)S(1)} %get-tuple-element.16.where, bf16[1,64,3,16,8,128]{5,4,3,2,1,0:T(8,128)(2,1)} %bitcast.33), custom_call_target="tpu_custom_call" | custom-call | tf_op jit(solution)/shard_map/pallas_call | solution.py:51
  3.6 1.4 %collective-permute-start.7 = (bf16[2,2,64,1536]{3,2,1,0:T(8,128)(2,1)S(1)}, bf16[2,2,64,1536]{3,2,1,0:T(8,128)(2,1)S(1)}, u32[]{:S(2)}, u32[]{:S(2)}) collective-permute-start(bf16[2,2,64,1536]{3,2,1,0:T(8,128)(2,1)S(1)} %shard_map.28), channel_id=1, source_target_pairs={{0,8},{1,9},{2,10},{3,11},{4,12},{5,13},{6,14},{7,15},{8,0},{9,1},... | collective-permute-start | bytes 2359304 | tf_op jit(solution)/shard_map/ppermute | solution.py:165
  4.9 2.1 %shard_map.29 = bf16[2,2,64,1536]{3,2,1,0:T(8,128)(2,1)S(1)} custom-call(s32[2]{0:T(128)S(1)} %get-tuple-element.17.where, bf16[1,64,3,16,8,128]{5,4,3,2,1,0:T(8,128)(2,1)} %bitcast.34), custom_call_target="tpu_custom_call" | custom-call | tf_op jit(solution)/shard_map/pallas_call | solution.py:51
  7.0 3.0 %collective-permute-start.6 = (bf16[2,2,64,1536]{3,2,1,0:T(8,128)(2,1)S(1)}, bf16[2,2,64,1536]{3,2,1,0:T(8,128)(2,1)S(1)}, u32[]{:S(2)}, u32[]{:S(2)}) collective-permute-start(bf16[2,2,64,1536]{3,2,1,0:T(8,128)(2,1)S(1)} %shard_map.29), channel_id=1, source_target_pairs={{0,4},{1,5},{2,6},{3,7},{4,0},{5,1},{6,2},{7,3},{8,12},{9,13},{10,... | collective-permute-start | bytes 2359304 | tf_op jit(solution)/shard_map/ppermute | solution.py:165
  10.0 0.1 pad_add_fusion.1.where
  10.1 3.4 %shard_map.30 = (bf16[2,2,64,1536]{3,2,1,0:T(8,128)(2,1)}, bf16[2,2,64,1536]{3,2,1,0:T(8,128)(2,1)}) custom-call(s32[3]{0:T(128)S(1)} %pad_add_fusion.1.where, bf16[1,64,3,16,8,128]{5,4,3,2,1,0:T(8,128)(2,1)} %bitcast.35, bf16[1,64,3,16,8,128]{5,4,3,2,1,0:T(8,128)(2,1)} %bitcast.36), custom_call_target="tpu_custom_call" | custom-call | tf_op jit(solution)/shard_map/pallas_call | solution.py:51
  13.5 0.4 collective-permute-start.5
  13.9 3.2 %collective-permute-start.4 = (bf16[2,2,64,1536]{3,2,1,0:T(8,128)(2,1)}, bf16[2,2,64,1536]{3,2,1,0:T(8,128)(2,1)}, u32[]{:S(2)}, u32[]{:S(2)}) collective-permute-start(bf16[2,2,64,1536]{3,2,1,0:T(8,128)(2,1)} %get-tuple-element.19), channel_id=1, source_target_pairs={{0,14},{1,15},{2,8},{3,9},{4,10},{5,11},{6,12},{7,13},{8,6},{9,7},... | collective-permute-start | bytes 2359304 | tf_op jit(solution)/shard_map/ppermute | solution.py:165
  17.1 0.1 stack.75.where
  17.2 4.8 %shard_map.31 = (bf16[2,2,64,1536]{3,2,1,0:T(8,128)(2,1)}, bf16[2,2,64,1536]{3,2,1,0:T(8,128)(2,1)}, bf16[2,2,64,1536]{3,2,1,0:T(8,128)(2,1)}, bf16[2,2,64,1536]{3,2,1,0:T(8,128)(2,1)}) custom-call(s32[5]{0:T(128)S(1)} %stack.75.where, bf16[1,64,3,16,8,128]{5,4,3,2,1,0:T(8,128)(2,1)} %bitcast.37, bf16[1,64,3,16,8,128]{5,4,3,2,1,0:T(8,128)(2,1)} %bitcast.38, ...), custom_call_target="tpu_custom_call" | custom-call | tf_op jit(solution)/shard_map/pallas_call | solution.py:51
  21.9 0.9 collective-permute-done.7.refs_0_
  22.8 2.8 %collective-permute-start.1 = (bf16[2,2,64,1536]{3,2,1,0:T(8,128)(2,1)}, bf16[2,2,64,1536]{3,2,1,0:T(8,128)(2,1)S(1)}, u32[]{:S(2)}, u32[]{:S(2)}) collective-permute-start(bf16[2,2,64,1536]{3,2,1,0:T(8,128)(2,1)} %get-tuple-element.23), channel_id=1, source_target_pairs={{0,6},{1,7},{2,0},{3,1},{4,2},{5,3},{6,4},{7,5},{8,14},{9,15},{10,... | collective-permute-start | bytes 2359304 | tf_op jit(solution)/shard_map/ppermute | solution.py:165
  25.6 18.7 %collective-permute-done.6.refs_0_ = bf16[2,2,64,1536]{3,2,1,0:T(8,128)(2,1)S(1)} collective-permute-done((bf16[2,2,64,1536]{3,2,1,0:T(8,128)(2,1)S(1)}, bf16[2,2,64,1536]{3,2,1,0:T(8,128)(2,1)S(1)}, u32[]{:S(2)}, u32[]{:S(2)}) %collective-permute-start.6) | collective-permute-done | bytes 786464 | tf_op jit(solution)/shard_map/ppermute | solution.py:165
  44.3 0.0 copy-start.2
  44.3 0.9 copy-done.2
  45.2 0.0 collective-permute-start.2
  45.2 0.0 collective-permute-done
  45.2 3.0 %collective-permute-start.3 = (bf16[2,2,64,1536]{3,2,1,0:T(8,128)(2,1)}, bf16[2,2,64,1536]{3,2,1,0:T(8,128)(2,1)S(1)}, u32[]{:S(2)}, u32[]{:S(2)}) collective-permute-start(bf16[2,2,64,1536]{3,2,1,0:T(8,128)(2,1)} %get-tuple-element.25), channel_id=1, source_target_pairs={{0,12},{1,13},{2,14},{3,15},{4,8},{5,9},{6,10},{7,11},{8,4},{9,5},... | collective-permute-start | bytes 2359304 | tf_op jit(solution)/shard_map/ppermute | solution.py:165
  48.2 9.0 %shard_map.32.near = bf16[8,2,128,1536]{3,2,1,0:T(8,128)(2,1)} custom-call(s32[1]{0:T(128)} %bitcast.3.where, bf16[16,128,3,1,8,128]{5,4,3,2,1,0:T(8,128)(2,1)} %bitcast.41), custom_call_target="tpu_custom_call" | custom-call | tf_op jit(solution)/shard_map/pallas_call | solution.py:73
  57.1 0.1 pad_add_fusion.where
  57.2 0.0 copy-start
  57.2 0.0 copy-start.4
  57.2 10.1 %shard_map.33.far = bf16[8,2,128,1536]{3,2,1,0:T(8,128)(2,1)} custom-call(s32[1]{0:T(128)} %bitcast.3.where, bf16[16,128,3,1,8,128]{5,4,3,2,1,0:T(8,128)(2,1)} %bitcast.20.src), custom_call_target="tpu_custom_call" | custom-call | tf_op jit(solution)/shard_map/pallas_call | solution.py:73
  67.3 0.0 copy-done
  67.3 0.0 copy-done.4
  67.3 0.0 copy-start.1
  67.3 2.8 %copy-done.1 = bf16[8,2,128,1536]{3,2,1,0:T(8,128)(2,1)S(1)} copy-done((bf16[8,2,128,1536]{3,2,1,0:T(8,128)(2,1)S(1)}, bf16[8,2,128,1536]{3,2,1,0:T(8,128)(2,1)}, u32[]{:S(2)}) %copy-start.1) | copy-done | bytes 6291480
  70.1 0.6 shard_map.34.refs_1_
  70.7 0.0 copy-start.3
  70.7 0.6 shard_map.35.refs_1_
  71.4 0.5 copy-done.3
  71.8 0.6 shard_map.36.refs_1_
  72.5 0.0 collective-permute-done.5.refs_0_
  72.5 1.8 %shard_map.37.refs_1_ = f32[16,8,8,128]{3,2,1,0:T(8,128)S(1)} custom-call(s32[1]{0:T(128)} %bitcast.22.where, bf16[8,2,128,1536]{3,2,1,0:T(8,128)(2,1)S(1)} %copy-done, bf16[8,2,128,1536]{3,2,1,0:T(8,128)(2,1)S(1)} %copy-done.1, bf16[2,2,64,1536]{3,2,1,0:T(8,128)(2,1)} %collective-permute-done.5.refs_0_, ...), custom_call_target="tpu_custom_call", output_to_operand_aliasing={{}: (4, {})} | custom-call | tf_op jit(solution)/shard_map/pallas_call | solution.py:119
  74.3 0.0 collective-permute-done.4.refs_0_
  74.3 1.8 %shard_map.38.refs_3_ = f32[16,8,8,128]{3,2,1,0:T(8,128)S(1)} custom-call(s32[1]{0:T(128)} %bitcast.21.where, bf16[8,2,128,1536]{3,2,1,0:T(8,128)(2,1)S(1)} %copy-done, bf16[8,2,128,1536]{3,2,1,0:T(8,128)(2,1)S(1)} %copy-done.1, bf16[2,2,64,1536]{3,2,1,0:T(8,128)(2,1)} %collective-permute-done.4.refs_0_, ...), custom_call_target="tpu_custom_call", output_to_operand_aliasing={{}: (4, {})} | custom-call | tf_op jit(solution)/shard_map/pallas_call | solution.py:119
  76.1 2.3 %collective-permute-done.1.refs_0_ = bf16[2,2,64,1536]{3,2,1,0:T(8,128)(2,1)S(1)} collective-permute-done((bf16[2,2,64,1536]{3,2,1,0:T(8,128)(2,1)}, bf16[2,2,64,1536]{3,2,1,0:T(8,128)(2,1)S(1)}, u32[]{:S(2)}, u32[]{:S(2)}) %collective-permute-start.1) | collective-permute-done | bytes 786464 | tf_op jit(solution)/shard_map/ppermute | solution.py:165
  78.3 3.0 %collective-permute-done.2.refs_1_ = bf16[2,2,64,1536]{3,2,1,0:T(8,128)(2,1)S(1)} collective-permute-done((bf16[2,2,64,1536]{3,2,1,0:T(8,128)(2,1)}, bf16[2,2,64,1536]{3,2,1,0:T(8,128)(2,1)S(1)}, u32[]{:S(2)}, u32[]{:S(2)}) %collective-permute-start.2) | collective-permute-done | bytes 786464 | tf_op jit(solution)/shard_map/ppermute | solution.py:165
  81.4 0.0 collective-permute-done.3.refs_2_
  81.4 2.6 %shard_map.39 = f32[16,8,8,128]{3,2,1,0:T(8,128)S(1)} custom-call(s32[3]{0:T(128)S(1)} %pad_add_fusion.where, bf16[8,2,128,1536]{3,2,1,0:T(8,128)(2,1)S(1)} %copy-done, bf16[8,2,128,1536]{3,2,1,0:T(8,128)(2,1)S(1)} %copy-done.1, bf16[2,2,64,1536]{3,2,1,0:T(8,128)(2,1)S(1)} %collective-permute-done.1.refs_0_, ...), custom_call_target="tpu_custom_call", output_to_operand_aliasing={{}: (6, {})} | custom-call | tf_op jit(solution)/shard_map/pallas_call | solution.py:119
  84.0 15.0 %all_to_all.5 = f32[16,8,8,128]{3,2,1,0:T(8,128)S(1)} all-to-all(f32[16,8,8,128]{3,2,1,0:T(8,128)S(1)} %shard_map.39), channel_id=1, replica_groups=mesh['tm'=8,'space'=16] {'space'}, dimensions={0} | all-to-all | bytes 1048576 | tf_op jit(solution)/shard_map/all_to_all | solution.py:180
  99.0 0.6 copy.17
  (1 shorter events, 0.0 us)
Async XLA Ops:
  0.0 45.2 %collective-permute-start = (bf16[16,128,2,3,512]{4,2,3,1,0:T(2,128)(2,1)}, bf16[16,128,2,3,512]{4,2,3,1,0:T(2,128)(2,1)}, u32[]{:S(2)}, u32[]{:S(2)}) collective-permute-start(bf16[16,128,2,3,512]{4,2,3,1,0:T(2,128)(2,1)} %param.3), channel_id=1, source_target_pairs={{0,1},{1,0},{2,3},{3,2},{4,5},{5,4},{6,7},{7,6},{8,9},{9,8},{10,11... | collective-permute-start | bytes 37748744 | tf_op jit(solution)/shard_map/ppermute | solution.py:172
  3.6 19.3 %collective-permute-start.7 = (bf16[2,2,64,1536]{3,2,1,0:T(8,128)(2,1)S(1)}, bf16[2,2,64,1536]{3,2,1,0:T(8,128)(2,1)S(1)}, u32[]{:S(2)}, u32[]{:S(2)}) collective-permute-start(bf16[2,2,64,1536]{3,2,1,0:T(8,128)(2,1)S(1)} %shard_map.28), channel_id=1, source_target_pairs={{0,8},{1,9},{2,10},{3,11},{4,12},{5,13},{6,14},{7,15},{8,0},{9,1},... | collective-permute-start | bytes 2359304 | tf_op jit(solution)/shard_map/ppermute | solution.py:165
  7.0 37.3 %collective-permute-start.6 = (bf16[2,2,64,1536]{3,2,1,0:T(8,128)(2,1)S(1)}, bf16[2,2,64,1536]{3,2,1,0:T(8,128)(2,1)S(1)}, u32[]{:S(2)}, u32[]{:S(2)}) collective-permute-start(bf16[2,2,64,1536]{3,2,1,0:T(8,128)(2,1)S(1)} %shard_map.29), channel_id=1, source_target_pairs={{0,4},{1,5},{2,6},{3,7},{4,0},{5,1},{6,2},{7,3},{8,12},{9,13},{10,... | collective-permute-start | bytes 2359304 | tf_op jit(solution)/shard_map/ppermute | solution.py:165
  13.5 59.0 %collective-permute-start.5 = (bf16[2,2,64,1536]{3,2,1,0:T(8,128)(2,1)}, bf16[2,2,64,1536]{3,2,1,0:T(8,128)(2,1)}, u32[]{:S(2)}, u32[]{:S(2)}) collective-permute-start(bf16[2,2,64,1536]{3,2,1,0:T(8,128)(2,1)} %get-tuple-element.26), channel_id=1, source_target_pairs={{0,10},{1,11},{2,12},{3,13},{4,14},{5,15},{6,8},{7,9},{8,2},{9,3},... | collective-permute-start | bytes 2359304 | tf_op jit(solution)/shard_map/ppermute | solution.py:165
  13.9 60.4 %collective-permute-start.4 = (bf16[2,2,64,1536]{3,2,1,0:T(8,128)(2,1)}, bf16[2,2,64,1536]{3,2,1,0:T(8,128)(2,1)}, u32[]{:S(2)}, u32[]{:S(2)}) collective-permute-start(bf16[2,2,64,1536]{3,2,1,0:T(8,128)(2,1)} %get-tuple-element.19), channel_id=1, source_target_pairs={{0,14},{1,15},{2,8},{3,9},{4,10},{5,11},{6,12},{7,13},{8,6},{9,7},... | collective-permute-start | bytes 2359304 | tf_op jit(solution)/shard_map/ppermute | solution.py:165
  22.8 55.5 %collective-permute-start.1 = (bf16[2,2,64,1536]{3,2,1,0:T(8,128)(2,1)}, bf16[2,2,64,1536]{3,2,1,0:T(8,128)(2,1)S(1)}, u32[]{:S(2)}, u32[]{:S(2)}) collective-permute-start(bf16[2,2,64,1536]{3,2,1,0:T(8,128)(2,1)} %get-tuple-element.23), channel_id=1, source_target_pairs={{0,6},{1,7},{2,0},{3,1},{4,2},{5,3},{6,4},{7,5},{8,14},{9,15},{10,... | collective-permute-start | bytes 2359304 | tf_op jit(solution)/shard_map/ppermute | solution.py:165
  44.3 0.9 copy-start.2
  45.2 36.2 %collective-permute-start.2 = (bf16[2,2,64,1536]{3,2,1,0:T(8,128)(2,1)}, bf16[2,2,64,1536]{3,2,1,0:T(8,128)(2,1)S(1)}, u32[]{:S(2)}, u32[]{:S(2)}) collective-permute-start(bf16[2,2,64,1536]{3,2,1,0:T(8,128)(2,1)} %get-tuple-element.24), channel_id=1, source_target_pairs={{0,2},{1,3},{2,4},{3,5},{4,6},{5,7},{6,0},{7,1},{8,10},{9,11},{10,... | collective-permute-start | bytes 2359304 | tf_op jit(solution)/shard_map/ppermute | solution.py:165
  45.2 36.2 %collective-permute-start.3 = (bf16[2,2,64,1536]{3,2,1,0:T(8,128)(2,1)}, bf16[2,2,64,1536]{3,2,1,0:T(8,128)(2,1)S(1)}, u32[]{:S(2)}, u32[]{:S(2)}) collective-permute-start(bf16[2,2,64,1536]{3,2,1,0:T(8,128)(2,1)} %get-tuple-element.25), channel_id=1, source_target_pairs={{0,12},{1,13},{2,14},{3,15},{4,8},{5,9},{6,10},{7,11},{8,4},{9,5},... | collective-permute-start | bytes 2359304 | tf_op jit(solution)/shard_map/ppermute | solution.py:165
  57.2 10.1 %copy-start = (bf16[8,2,128,1536]{3,2,1,0:T(8,128)(2,1)S(1)}, bf16[8,2,128,1536]{3,2,1,0:T(8,128)(2,1)}, u32[]{:S(2)}) copy-start(bf16[8,2,128,1536]{3,2,1,0:T(8,128)(2,1)} %shard_map.32.near) | copy-start | bytes 18874372
  57.2 10.1 %copy-start.4 = (bf16[2,2,64,1536]{3,2,1,0:T(8,128)(2,1)S(1)}, bf16[2,2,64,1536]{3,2,1,0:T(8,128)(2,1)}, u32[]{:S(2)}) copy-start(bf16[2,2,64,1536]{3,2,1,0:T(8,128)(2,1)} %get-tuple-element.21.refs_0_) | copy-start | bytes 2359300
  67.3 2.8 %copy-start.1 = (bf16[8,2,128,1536]{3,2,1,0:T(8,128)(2,1)S(1)}, bf16[8,2,128,1536]{3,2,1,0:T(8,128)(2,1)}, u32[]{:S(2)}) copy-start(bf16[8,2,128,1536]{3,2,1,0:T(8,128)(2,1)} %shard_map.33.far) | copy-start | bytes 18874372
  70.7 1.1 %copy-start.3 = (bf16[2,2,64,1536]{3,2,1,0:T(8,128)(2,1)S(1)}, bf16[2,2,64,1536]{3,2,1,0:T(8,128)(2,1)}, u32[]{:S(2)}) copy-start(bf16[2,2,64,1536]{3,2,1,0:T(8,128)(2,1)} %copy-done.2) | copy-start | bytes 2359300

commit v3 on v2

--- a/solution.py
+++ b/solution.py
@@ -6,18 +6,17 @@
 from jax.sharding import PartitionSpec as P
 
 LANES = 128
-VMEM = 16 * 2**20
-PACK_VMEM = 52 * 2**20
+VMEM = 8 * 2**20
 FREE = pl.CostEstimate(flops=0, bytes_accessed=0, transcendentals=0)
 RING = 4
-MOVES = [(1, 0), (0, 2), (1, 1), (1, 3), (0, 3), (0, 1), (1, 2)]
+MOVES = [(1, 2), (0, 2), (1, 0), (1, 1), (1, 3), (0, 3), (0, 1)]
 
 
 def tile_view(a, groups):
     outer, rows, parts, colors, sites = a.shape
     a = a.reshape(outer, rows, parts, colors, groups, sites // groups // LANES, LANES)
     a = a.transpose(0, 1, 3, 4, 5, 2, 6)
-    return a.reshape(outer, rows, colors, groups, -1, LANES)
+    return pltpu.with_memory_space_constraint(a.reshape(outer, rows, colors, groups, -1, LANES), pltpu.HBM)
 
 
 def split_lines(src, dst, wide, flip):
@@ -58,7 +57,7 @@
             scratch_shapes=[pltpu.VMEM((block_rows * (colors * 2 * inner + 8), LANES), jnp.float32)],
         ),
         out_shape=[jax.ShapeDtypeStruct((2, 2, rows, depth), view.dtype)] * count,
-        compiler_params=pltpu.CompilerParams(vmem_limit_bytes=PACK_VMEM),
+        compiler_params=pltpu.CompilerParams(vmem_limit_bytes=VMEM),
         cost_estimate=FREE,
     )(where, *[view] * count)
 
@@ -84,7 +83,7 @@
             scratch_shapes=[pltpu.VMEM((rows * colors * inner, LANES), jnp.float32)],
         ),
         out_shape=jax.ShapeDtypeStruct((times // 2, 2, rows, depth), view.dtype),
-        compiler_params=pltpu.CompilerParams(vmem_limit_bytes=PACK_VMEM),
+        compiler_params=pltpu.CompilerParams(vmem_limit_bytes=VMEM),
         cost_estimate=FREE,
     )(where, view)
 
@@ -165,11 +164,13 @@
         return {m: lax.ppermute(sends[m], "space", route(*m, 0)) for m in moves}
 
     done = core
-    for moves in (MOVES[:1], MOVES[1:2], MOVES[2:4], MOVES[4:] + [(0, 0)]):
+    for moves in (MOVES[:1], MOVES[1:3], MOVES[3:5], MOVES[5:] + [(0, 0)]):
         done = pack(moves, done)
+    raw = lax.optimization_barrier((eigvecs, sends[MOVES[0]]))[0]
+    swapped = lax.ppermute(raw, "space", route(0, 0, 1))
+    sends[MOVES[4]], swapped = lax.optimization_barrier((sends[MOVES[4]], swapped))
     arrived = send(MOVES)
     arrived[0, 0] = sends[0, 0]
-    swapped = lax.ppermute(eigvecs, "space", route(0, 0, 1))
     where = after([core], done)
     near = pack_vectors(vectors, where)
     far = pack_vectors(tile_view(swapped, 1), where)

time: 100 us -> 95.5 us (0.955)
  Pallas kernels: 39.4 us -> 34.6 us
  waiting for transfers between devices: 24.8 us -> 27.2 us
  local copies, waits for them, and re-layouts: 4.87 us -> 2.88 us
    pallas_call x2, Pallas kernels: 19 us -> 13.6 us  [pack_vectors(): pl.pallas_call(kernel, grid_spec=pltpu.PrefetchScalarGridSpec(num_scalar_...]
    unnamed x10 -> x8, local copies, waits for them, and re-layouts: 4.15 us -> 2.24 us
    ppermute x7, waiting for transfers between devices: 24.8 us -> 26.4 us  [send(): return {m: lax.ppermute(sends[m], 'space', route(*m, 0)) for m in moves}]
  transfers between devices with their start and end apart: 8 -> 8, of which waited for: 4 -> 4; matrix products, arithmetic and copies ran while one was open for 0% -> 0% of each run, Pallas kernels for 37% -> 32%
where the time goes in v3:
time: 95.5 us; the launch traced here: 94.9 us
  Pallas kernels  34.6 us (36%)
  waiting for transfers between devices  27.2 us (28%)
  starting transfers between devices  15.1 us (16%)
  blocking collectives  14.7 us (15%)
  local copies, waits for them, and re-layouts  2.88 us (3%)
    ppermute x7, waiting for transfers between devices, send(): return {m: lax.ppermute(sends[m], 'space', route(*m, 0)) for m in moves}  26.4 us
    all_to_all x1, blocking collectives, body(): lax.all_to_all(partial, 'space', split_axis=0, concat_axis=0, tiled=True)  14.7 us
    ppermute x7, starting transfers between devices, send(): return {m: lax.ppermute(sends[m], 'space', route(*m, 0)) for m in moves}  13.6 us
    pallas_call x2, Pallas kernels, pack_vectors(): pl.pallas_call(kernel, grid_spec=pltpu.PrefetchScalarGridSpec(num_scalar_...  13.6 us
    pallas_call x4, Pallas kernels, pack_solutions(): pl.pallas_call(kernel, grid_spec=pltpu.PrefetchScalarGridSpec(num_scalar_...  12.9 us
    pallas_call x6, Pallas kernels, product(): pl.pallas_call(kernel, grid_spec=pltpu.PrefetchScalarGridSpec(num_scalar_...  8.08 us
    unnamed x8, local copies, waits for them, and re-layouts  2.24 us
  transfers between devices with their start and end apart: 8, of which 4 were waited for; matrix products, arithmetic and copies ran while one was open for 0% of the time, Pallas kernels for 32%

profile of v3, /device:TPU:1, one launch (start us, length us, event | category | flops | bytes accessed | tf_op | source)
XLA Modules:
  0.0 94.9 jit_solution(7875519512140650114)
XLA Ops:
  0.0 0.1 pad_add_fusion.2.where
  0.1 2.1 %shard_map.28 = bf16[2,2,64,1536]{3,2,1,0:T(8,128)(2,1)S(1)} custom-call(s32[2]{0:T(128)S(1)} %pad_add_fusion.2.where, bf16[1,64,3,16,8,128]{5,4,3,2,1,0:T(8,128)(2,1)} %bitcast.33), custom_call_target="tpu_custom_call" | custom-call | tf_op jit(solution)/shard_map/pallas_call | solution.py:50
  2.1 1.5 %collective-permute-start = (bf16[16,128,2,3,512]{4,2,3,1,0:T(2,128)(2,1)}, bf16[16,128,2,3,512]{4,2,3,1,0:T(2,128)(2,1)}, u32[]{:S(2)}, u32[]{:S(2)}) collective-permute-start(bf16[16,128,2,3,512]{4,2,3,1,0:T(2,128)(2,1)} %param.3), channel_id=1, source_target_pairs={{0,1},{1,0},{2,3},{3,2},{4,5},{5,4},{6,7},{7,6},{8,9},{9,8},{10,11... | collective-permute-start | bytes 37748744 | tf_op jit(solution)/shard_map/ppermute | solution.py:170
  3.6 3.9 %collective-permute-start.7 = (bf16[2,2,64,1536]{3,2,1,0:T(8,128)(2,1)S(1)}, bf16[2,2,64,1536]{3,2,1,0:T(8,128)(2,1)S(1)}, u32[]{:S(2)}, u32[]{:S(2)}) collective-permute-start(bf16[2,2,64,1536]{3,2,1,0:T(8,128)(2,1)S(1)} %shard_map.28), channel_id=1, source_target_pairs={{0,12},{1,13},{2,14},{3,15},{4,8},{5,9},{6,10},{7,11},{8,4},{9,5},... | collective-permute-start | bytes 2359304 | tf_op jit(solution)/shard_map/ppermute | solution.py:164
  7.6 0.1 add_add_fusion
  7.7 3.4 %shard_map.29 = (bf16[2,2,64,1536]{3,2,1,0:T(8,128)(2,1)}, bf16[2,2,64,1536]{3,2,1,0:T(8,128)(2,1)}) custom-call(s32[3]{0:T(128)S(1)} %get-tuple-element.21.where, bf16[1,64,3,16,8,128]{5,4,3,2,1,0:T(8,128)(2,1)} %bitcast.34, bf16[1,64,3,16,8,128]{5,4,3,2,1,0:T(8,128)(2,1)} %bitcast.35), custom_call_target="tpu_custom_call" | custom-call | tf_op jit(solution)/shard_map/pallas_call | solution.py:50
  11.1 0.1 collective-permute-start.6
  11.1 0.2 collective-permute-start.5
  11.3 3.4 %shard_map.30 = (bf16[2,2,64,1536]{3,2,1,0:T(8,128)(2,1)}, bf16[2,2,64,1536]{3,2,1,0:T(8,128)(2,1)}) custom-call(s32[3]{0:T(128)S(1)} %get-tuple-element.23.where, bf16[1,64,3,16,8,128]{5,4,3,2,1,0:T(8,128)(2,1)} %bitcast.36, bf16[1,64,3,16,8,128]{5,4,3,2,1,0:T(8,128)(2,1)} %bitcast.37), custom_call_target="tpu_custom_call" | custom-call | tf_op jit(solution)/shard_map/pallas_call | solution.py:50
  14.8 2.3 %collective-permute-start.4 = (bf16[2,2,64,1536]{3,2,1,0:T(8,128)(2,1)}, bf16[2,2,64,1536]{3,2,1,0:T(8,128)(2,1)}, u32[]{:S(2)}, u32[]{:S(2)}) collective-permute-start(bf16[2,2,64,1536]{3,2,1,0:T(8,128)(2,1)} %get-tuple-element.33), channel_id=1, source_target_pairs={{0,10},{1,11},{2,12},{3,13},{4,14},{5,15},{6,8},{7,9},{8,2},{9,3},... | collective-permute-start | bytes 2359304 | tf_op jit(solution)/shard_map/ppermute | solution.py:164
  17.0 0.1 pad_add_fusion.1.where
  17.1 4.0 %shard_map.31 = (bf16[2,2,64,1536]{3,2,1,0:T(8,128)(2,1)}, bf16[2,2,64,1536]{3,2,1,0:T(8,128)(2,1)}, bf16[2,2,64,1536]{3,2,1,0:T(8,128)(2,1)S(1)}) custom-call(s32[4]{0:T(128)S(1)} %pad_add_fusion.1.where, bf16[1,64,3,16,8,128]{5,4,3,2,1,0:T(8,128)(2,1)} %bitcast.38, bf16[1,64,3,16,8,128]{5,4,3,2,1,0:T(8,128)(2,1)} %bitcast.39, ...), custom_call_target="tpu_custom_call" | custom-call | tf_op jit(solution)/shard_map/pallas_call | solution.py:50
  21.1 0.0 copy-start.2
  21.1 0.9 copy-done.2
  22.0 0.7 collective-permute-done
  22.8 2.8 %collective-permute-start.2 = (bf16[2,2,64,1536]{3,2,1,0:T(8,128)(2,1)}, bf16[2,2,64,1536]{3,2,1,0:T(8,128)(2,1)S(1)}, u32[]{:S(2)}, u32[]{:S(2)}) collective-permute-start(bf16[2,2,64,1536]{3,2,1,0:T(8,128)(2,1)} %get-tuple-element.31), channel_id=1, source_target_pairs={{0,6},{1,7},{2,0},{3,1},{4,2},{5,3},{6,4},{7,5},{8,14},{9,15},{10,... | collective-permute-start | bytes 2359304 | tf_op jit(solution)/shard_map/ppermute | solution.py:164
  25.6 0.0 collective-permute-done.7.refs_0_
  25.6 1.0 %collective-permute-start.3 = (bf16[2,2,64,1536]{3,2,1,0:T(8,128)(2,1)}, bf16[2,2,64,1536]{3,2,1,0:T(8,128)(2,1)S(1)}, u32[]{:S(2)}, u32[]{:S(2)}) collective-permute-start(bf16[2,2,64,1536]{3,2,1,0:T(8,128)(2,1)} %get-tuple-element.32), channel_id=1, source_target_pairs={{0,2},{1,3},{2,4},{3,5},{4,6},{5,7},{6,0},{7,1},{8,10},{9,11},{10,... | collective-permute-start | bytes 2359304 | tf_op jit(solution)/shard_map/ppermute | solution.py:164
  26.6 16.3 %collective-permute-done.6.refs_0_ = bf16[2,2,64,1536]{3,2,1,0:T(8,128)(2,1)S(1)} collective-permute-done((bf16[2,2,64,1536]{3,2,1,0:T(8,128)(2,1)}, bf16[2,2,64,1536]{3,2,1,0:T(8,128)(2,1)S(1)}, u32[]{:S(2)}, u32[]{:S(2)}) %collective-permute-start.6) | collective-permute-done | bytes 786464 | tf_op jit(solution)/shard_map/ppermute | solution.py:164
  42.8 0.0 copy-start
  42.8 0.9 copy-done
  43.7 3.4 %collective-permute-start.1 = (bf16[2,2,64,1536]{3,2,1,0:T(8,128)(2,1)}, bf16[2,2,64,1536]{3,2,1,0:T(8,128)(2,1)S(1)}, u32[]{:S(2)}, u32[]{:S(2)}) collective-permute-start(bf16[2,2,64,1536]{3,2,1,0:T(8,128)(2,1)} %get-tuple-element.30), channel_id=1, source_target_pairs={{0,14},{1,15},{2,8},{3,9},{4,10},{5,11},{6,12},{7,13},{8,6},{9,7},... | collective-permute-start | bytes 2359304 | tf_op jit(solution)/shard_map/ppermute | solution.py:164
  47.1 6.8 %shard_map.32.near = bf16[8,2,128,1536]{3,2,1,0:T(8,128)(2,1)S(1)} custom-call(s32[1]{0:T(128)} %bitcast.3.where, bf16[16,128,3,1,8,128]{5,4,3,2,1,0:T(8,128)(2,1)} %bitcast.41), custom_call_target="tpu_custom_call" | custom-call | tf_op jit(solution)/shard_map/pallas_call | solution.py:72
  53.8 0.1 pad_add_fusion.where
  53.9 0.0 copy-start.3
  53.9 6.8 %shard_map.33.far = bf16[8,2,128,1536]{3,2,1,0:T(8,128)(2,1)S(1)} custom-call(s32[1]{0:T(128)} %bitcast.3.where, bf16[16,128,3,1,8,128]{5,4,3,2,1,0:T(8,128)(2,1)} %bitcast.20.src), custom_call_target="tpu_custom_call" | custom-call | tf_op jit(solution)/shard_map/pallas_call | solution.py:72
  60.8 0.0 copy-done.3
  60.8 0.6 shard_map.34.refs_1_
  61.4 0.0 copy-start.1
  61.4 0.7 shard_map.35.refs_1_
  62.1 0.5 copy-done.1
  62.6 0.6 shard_map.36.refs_1_
  63.2 0.0 collective-permute-done.5.refs_0_
  63.2 1.8 %shard_map.37.refs_1_ = f32[16,8,8,128]{3,2,1,0:T(8,128)S(1)} custom-call(s32[1]{0:T(128)} %bitcast.10.where, bf16[8,2,128,1536]{3,2,1,0:T(8,128)(2,1)S(1)} %shard_map.32.near, bf16[8,2,128,1536]{3,2,1,0:T(8,128)(2,1)S(1)} %shard_map.33.far, bf16[2,2,64,1536]{3,2,1,0:T(8,128)(2,1)} %collective-permute-done.5.refs_0_, ...), custom_call_target="tpu_custom_call", output_to_operand_aliasing={{}: (4, {})} | custom-call | tf_op jit(solution)/shard_map/pallas_call | solution.py:118
  65.0 0.0 collective-permute-done.4.refs_0_
  65.0 1.8 %shard_map.38.refs_3_ = f32[16,8,8,128]{3,2,1,0:T(8,128)S(1)} custom-call(s32[1]{0:T(128)} %bitcast.21.where, bf16[8,2,128,1536]{3,2,1,0:T(8,128)(2,1)S(1)} %shard_map.32.near, bf16[8,2,128,1536]{3,2,1,0:T(8,128)(2,1)S(1)} %shard_map.33.far, bf16[2,2,64,1536]{3,2,1,0:T(8,128)(2,1)} %collective-permute-done.4.refs_0_, ...), custom_call_target="tpu_custom_call", output_to_operand_aliasing={{}: (4, {})} | custom-call | tf_op jit(solution)/shard_map/pallas_call | solution.py:118
  66.8 0.0 collective-permute-done.2.refs_1_
  66.8 9.3 %collective-permute-done.3.refs_2_ = bf16[2,2,64,1536]{3,2,1,0:T(8,128)(2,1)S(1)} collective-permute-done((bf16[2,2,64,1536]{3,2,1,0:T(8,128)(2,1)}, bf16[2,2,64,1536]{3,2,1,0:T(8,128)(2,1)S(1)}, u32[]{:S(2)}, u32[]{:S(2)}) %collective-permute-start.3) | collective-permute-done | bytes 786464 | tf_op jit(solution)/shard_map/ppermute | solution.py:164
  76.1 0.8 collective-permute-done.1.refs_0_
  77.0 2.6 %shard_map.39 = f32[16,8,8,128]{3,2,1,0:T(8,128)S(1)} custom-call(s32[3]{0:T(128)S(1)} %pad_add_fusion.where, bf16[8,2,128,1536]{3,2,1,0:T(8,128)(2,1)S(1)} %shard_map.32.near, bf16[8,2,128,1536]{3,2,1,0:T(8,128)(2,1)S(1)} %shard_map.33.far, bf16[2,2,64,1536]{3,2,1,0:T(8,128)(2,1)S(1)} %collective-permute-done.1.refs_0_, ...), custom_call_target="tpu_custom_call", output_to_operand_aliasing={{}: (6, {})} | custom-call | tf_op jit(solution)/shard_map/pallas_call | solution.py:118
  79.5 14.7 %all_to_all.5 = f32[16,8,8,128]{3,2,1,0:T(8,128)S(1)} all-to-all(f32[16,8,8,128]{3,2,1,0:T(8,128)S(1)} %shard_map.39), channel_id=1, replica_groups=mesh['tm'=8,'space'=16] {'space'}, dimensions={0} | all-to-all | bytes 1048576 | tf_op jit(solution)/shard_map/all_to_all | solution.py:181
  94.3 0.6 copy.17
  (1 shorter events, 0.0 us)
Async XLA Ops:
  2.1 20.6 %collective-permute-start = (bf16[16,128,2,3,512]{4,2,3,1,0:T(2,128)(2,1)}, bf16[16,128,2,3,512]{4,2,3,1,0:T(2,128)(2,1)}, u32[]{:S(2)}, u32[]{:S(2)}) collective-permute-start(bf16[16,128,2,3,512]{4,2,3,1,0:T(2,128)(2,1)} %param.3), channel_id=1, source_target_pairs={{0,1},{1,0},{2,3},{3,2},{4,5},{5,4},{6,7},{7,6},{8,9},{9,8},{10,11... | collective-permute-start | bytes 37748744 | tf_op jit(solution)/shard_map/ppermute | solution.py:170
  3.6 21.9 %collective-permute-start.7 = (bf16[2,2,64,1536]{3,2,1,0:T(8,128)(2,1)S(1)}, bf16[2,2,64,1536]{3,2,1,0:T(8,128)(2,1)S(1)}, u32[]{:S(2)}, u32[]{:S(2)}) collective-permute-start(bf16[2,2,64,1536]{3,2,1,0:T(8,128)(2,1)S(1)} %shard_map.28), channel_id=1, source_target_pairs={{0,12},{1,13},{2,14},{3,15},{4,8},{5,9},{6,10},{7,11},{8,4},{9,5},... | collective-permute-start | bytes 2359304 | tf_op jit(solution)/shard_map/ppermute | solution.py:164
  11.1 31.8 %collective-permute-start.6 = (bf16[2,2,64,1536]{3,2,1,0:T(8,128)(2,1)}, bf16[2,2,64,1536]{3,2,1,0:T(8,128)(2,1)S(1)}, u32[]{:S(2)}, u32[]{:S(2)}) collective-permute-start(bf16[2,2,64,1536]{3,2,1,0:T(8,128)(2,1)} %get-tuple-element.34), channel_id=1, source_target_pairs={{0,4},{1,5},{2,6},{3,7},{4,0},{5,1},{6,2},{7,3},{8,12},{9,13},{10,... | collective-permute-start | bytes 2359304 | tf_op jit(solution)/shard_map/ppermute | solution.py:164
  11.1 52.1 %collective-permute-start.5 = (bf16[2,2,64,1536]{3,2,1,0:T(8,128)(2,1)}, bf16[2,2,64,1536]{3,2,1,0:T(8,128)(2,1)}, u32[]{:S(2)}, u32[]{:S(2)}) collective-permute-start(bf16[2,2,64,1536]{3,2,1,0:T(8,128)(2,1)} %get-tuple-element.22), channel_id=1, source_target_pairs={{0,8},{1,9},{2,10},{3,11},{4,12},{5,13},{6,14},{7,15},{8,0},{9,1},... | collective-permute-start | bytes 2359304 | tf_op jit(solution)/shard_map/ppermute | solution.py:164
  14.8 50.2 %collective-permute-start.4 = (bf16[2,2,64,1536]{3,2,1,0:T(8,128)(2,1)}, bf16[2,2,64,1536]{3,2,1,0:T(8,128)(2,1)}, u32[]{:S(2)}, u32[]{:S(2)}) collective-permute-start(bf16[2,2,64,1536]{3,2,1,0:T(8,128)(2,1)} %get-tuple-element.33), channel_id=1, source_target_pairs={{0,10},{1,11},{2,12},{3,13},{4,14},{5,15},{6,8},{7,9},{8,2},{9,3},... | collective-permute-start | bytes 2359304 | tf_op jit(solution)/shard_map/ppermute | solution.py:164
  21.1 0.9 copy-start.2
  22.8 44.0 %collective-permute-start.2 = (bf16[2,2,64,1536]{3,2,1,0:T(8,128)(2,1)}, bf16[2,2,64,1536]{3,2,1,0:T(8,128)(2,1)S(1)}, u32[]{:S(2)}, u32[]{:S(2)}) collective-permute-start(bf16[2,2,64,1536]{3,2,1,0:T(8,128)(2,1)} %get-tuple-element.31), channel_id=1, source_target_pairs={{0,6},{1,7},{2,0},{3,1},{4,2},{5,3},{6,4},{7,5},{8,14},{9,15},{10,... | collective-permute-start | bytes 2359304 | tf_op jit(solution)/shard_map/ppermute | solution.py:164
  25.6 50.5 %collective-permute-start.3 = (bf16[2,2,64,1536]{3,2,1,0:T(8,128)(2,1)}, bf16[2,2,64,1536]{3,2,1,0:T(8,128)(2,1)S(1)}, u32[]{:S(2)}, u32[]{:S(2)}) collective-permute-start(bf16[2,2,64,1536]{3,2,1,0:T(8,128)(2,1)} %get-tuple-element.32), channel_id=1, source_target_pairs={{0,2},{1,3},{2,4},{3,5},{4,6},{5,7},{6,0},{7,1},{8,10},{9,11},{10,... | collective-permute-start | bytes 2359304 | tf_op jit(solution)/shard_map/ppermute | solution.py:164
  42.8 0.9 copy-start
  43.7 33.2 %collective-permute-start.1 = (bf16[2,2,64,1536]{3,2,1,0:T(8,128)(2,1)}, bf16[2,2,64,1536]{3,2,1,0:T(8,128)(2,1)S(1)}, u32[]{:S(2)}, u32[]{:S(2)}) collective-permute-start(bf16[2,2,64,1536]{3,2,1,0:T(8,128)(2,1)} %get-tuple-element.30), channel_id=1, source_target_pairs={{0,14},{1,15},{2,8},{3,9},{4,10},{5,11},{6,12},{7,13},{8,6},{9,7},... | collective-permute-start | bytes 2359304 | tf_op jit(solution)/shard_map/ppermute | solution.py:164
  53.9 6.9 %copy-start.3 = (bf16[2,2,64,1536]{3,2,1,0:T(8,128)(2,1)S(1)}, bf16[2,2,64,1536]{3,2,1,0:T(8,128)(2,1)}, u32[]{:S(2)}) copy-start(bf16[2,2,64,1536]{3,2,1,0:T(8,128)(2,1)} %copy-done.2) | copy-start | bytes 2359300
  61.4 1.1 %copy-start.1 = (bf16[2,2,64,1536]{3,2,1,0:T(8,128)(2,1)S(1)}, bf16[2,2,64,1536]{3,2,1,0:T(8,128)(2,1)}, u32[]{:S(2)}) copy-start(bf16[2,2,64,1536]{3,2,1,0:T(8,128)(2,1)} %copy-done) | copy-start | bytes 2359300

commit v4 on v3

v4 whole, which is shorter than its diff:
```python
import jax
import jax.numpy as jnp
from jax import lax
from jax.experimental import pallas as pl
from jax.experimental.pallas import tpu as pltpu
from jax.sharding import PartitionSpec as P

LANES = 128
VMEM = 8 * 2**20
FREE = pl.CostEstimate(flops=0, bytes_accessed=0, transcendentals=0)
RING = 4
MOVES = [(1, 2), (0, 2), (1, 0), (1, 1), (1, 3), (0, 3), (0, 1)]
LAST = [(0, 3), (1, 3), (0, 1)]


def tile_view(a, groups):
    outer, rows, parts, colors, sites = a.shape
    a = a.reshape(outer, rows, parts, colors, groups, sites // groups // LANES, LANES)
    a = a.transpose(0, 1, 3, 4, 5, 2, 6)
    return a.reshape(outer, rows, colors, groups, -1, LANES)


def split_lines(src, dst, wide, flip):
    _, rows, colors, groups, inner, _ = src.shape
    lines = colors * groups * inner
    stride = wide.shape[0] // rows
    for i in range(rows):
        wide[i * stride : i * stride + lines] = src[0, i].astype(jnp.float32).reshape(lines, LANES)
    for g in range(groups):
        for c in range(colors):
            for k in range(inner):
                picked = wide[pl.ds((c * groups + g) * inner + k, rows, stride=stride), :]
                lane = (c * (inner // 2) + k // 2) * LANES
                dst[g ^ flip, k % 2, :, pl.ds(lane, LANES)] = picked.astype(jnp.bfloat16)


def here():
    me = lax.axis_index("space")
    return me // (2 * RING), me // 2 % RING, me % 2


def chip_at(dx, dy):
    x, y, _ = here()
    return (x ^ dx) * RING + (y + dy) % RING


def pack_solutions(view, moves, block_rows=32):
    _, rows, colors, groups, inner, _ = view.shape
    count = len(moves)
    depth = colors * inner // 2 * LANES

    def kernel(*refs):
        for n in range(count):
            split_lines(refs[n], refs[count + n], refs[2 * count], here()[2])

    def source(move):
        return pl.BlockSpec(
            (1, block_rows, colors, 2, inner, LANES), lambda b: (0, b, 0, chip_at(*move), 0, 0)
        )

    return pl.pallas_call(
        kernel,
        grid=(rows // block_rows,),
        in_specs=[source(m) for m in moves],
        out_specs=[pl.BlockSpec((2, 2, block_rows, depth), lambda b: (0, 0, b, 0))] * count,
        scratch_shapes=[pltpu.VMEM((block_rows * (colors * 2 * inner + 8), LANES), jnp.float32)],
        out_shape=[jax.ShapeDtypeStruct((2, 2, rows, depth), view.dtype)] * count,
        compiler_params=pltpu.CompilerParams(vmem_limit_bytes=VMEM),
        cost_estimate=FREE,
    )(*[view] * count)


def pack_vectors(view):
    times, rows, colors, _, inner, _ = view.shape
    depth = colors * inner // 2 * LANES

    def kernel(src, dst, wide):
        split_lines(src, dst, wide, 0)

    return pl.pallas_call(
        kernel,
        grid=(times // 2,),
        in_specs=[
            pl.BlockSpec((1, rows, colors, 1, inner, LANES), lambda t: (2 * t + here()[2], 0, 0, 0, 0, 0))
        ],
        out_specs=pl.BlockSpec((1, 2, rows, depth), lambda t: (t, 0, 0, 0)),
        scratch_shapes=[pltpu.VMEM((rows * colors * inner, LANES), jnp.float32)],
        out_shape=jax.ShapeDtypeStruct((times // 2, 2, rows, depth), view.dtype),
        compiler_params=pltpu.CompilerParams(vmem_limit_bytes=VMEM),
        cost_estimate=FREE,
    )(view)


def product(near, far, sol, move, partial, shares):
    times, _, rows, depth = near.shape
    cols = sol.shape[2]
    held = [] if partial is None else [partial]

    def time():
        return chip_at(move[0], -move[1])

    def kernel(near, far, sol, *refs):
        out = refs[-1]
        g = jnp.zeros((2 * rows, 2 * cols), jnp.float32)
        for h, vec in enumerate((near, far)):
            g += lax.dot_general(
                vec[0].reshape(2 * rows, depth),
                sol[h].reshape(2 * cols, depth),
                (((1,), (1,)), ((), ())),
                preferred_element_type=jnp.float32,
            )
        crossed = pltpu.roll(g[rows:], cols, 1)
        lane = lax.broadcasted_iota(jnp.int32, crossed.shape, 1)
        out[...] = (g[:rows] + jnp.where(lane < cols, crossed, -crossed)).reshape(out.shape)

    vec_spec = pl.BlockSpec((1, 2, rows, depth), lambda i: (time(), 0, 0, 0))
    return pl.pallas_call(
        kernel,
        grid=(1,),
        in_specs=[vec_spec, vec_spec, pl.BlockSpec(sol.shape, lambda i: (0, 0, 0, 0))]
        + [pl.BlockSpec(memory_space=pl.ANY)] * len(held),
        out_specs=pl.BlockSpec((shares, 1, rows // shares, 2 * cols), lambda i: (0, time(), 0, 0)),
        out_shape=jax.ShapeDtypeStruct((shares, times, rows // shares, 2 * cols), jnp.float32),
        input_output_aliases={3: 0} if held else {},
        compiler_params=pltpu.CompilerParams(vmem_limit_bytes=VMEM),
        cost_estimate=FREE,
    )(near, far, sol, *held)


def body(solutions, eigvecs):
    shares = lax.axis_size("space")
    chips = shares // 2
    def route(dx, dy, dc):
        return [
            (i, (((i // 2 // RING) ^ dx) * RING + (i // 2 + dy) % RING) * 2 + (i % 2 ^ dc))
            for i in range(shares)
        ]

    def held_view(a, groups, done):
        a = lax.optimization_barrier((a, done))[0] if done is not None else a
        return pltpu.with_memory_space_constraint(tile_view(a, groups), pltpu.HBM)

    sends = {}
    done = None
    for moves in (MOVES[:1], MOVES[1:3], MOVES[3:5], MOVES[5:] + [(0, 0)]):
        chunks = pack_solutions(held_view(solutions, shares, done), moves)
        sends.update(zip(moves, chunks))
        done = chunks[-1]
    raw = lax.optimization_barrier((eigvecs, sends[MOVES[0]]))[0]
    swapped = lax.ppermute(raw, "space", route(0, 0, 1))
    sends[MOVES[4]], swapped = lax.optimization_barrier((sends[MOVES[4]], swapped))
    arrived = {m: lax.ppermute(sends[m], "space", route(*m, 0)) for m in MOVES}
    arrived[0, 0] = sends[0, 0]
    near = pack_vectors(held_view(eigvecs, 1, done))
    far = pack_vectors(tile_view(swapped, 1))
    partial = None
    for move in [(0, 0)] + MOVES[:4] + LAST:
        partial = product(near, far, arrived[move], move, partial, shares)
    partial = lax.all_to_all(partial, "space", split_axis=0, concat_axis=0, tiled=True)
    partial = partial.reshape(chips, 2, chips, -1, partial.shape[-1])
    total = jnp.sum(partial, axis=0)
    return jnp.swapaxes(total, 0, 1).reshape(shares, -1, total.shape[-1])


def solution(mesh):
    placed = (P(("tm", "space"), None, None, None, None), P("tm", None, None, None, "space"))
    return jax.shard_map(
        body, mesh=mesh, in_specs=placed, out_specs=P("tm", "space", None), check_vma=False
    )
```

time: 95.5 us -> 93.2 us (0.976)
  waiting for transfers between devices: 27.2 us -> 38.2 us
  Pallas kernels: 34.6 us -> 23.8 us
  local copies, waits for them, and re-layouts: 2.88 us -> 0.63 us
    pallas_call x12 -> x14, Pallas kernels: 34.6 us -> 23.8 us  [the longest x2 10.2 us: pack_vectors(): pl.pallas_call(kernel, grid=(times // 2,), in_specs=[pl.BlockSpec((1, row...]
    ppermute x7, waiting for transfers between devices: 26.4 us -> 32.8 us  [body(): arrived = {m: lax.ppermute(sends[m], 'space', route(*m, 0)) for m in MOVES}]
    ppermute x1, waiting for transfers between devices: 0.75 us -> 5.38 us  [body(): swapped = lax.ppermute(raw, 'space', route(0, 0, 1))]
    unnamed x8 -> x0, local copies, waits for them, and re-layouts: 2.24 us -> none
  transfers between devices with their start and end apart: 8 -> 8, of which waited for: 4 -> 4; matrix products, arithmetic and copies ran while one was open for 0% -> 0% of each run, Pallas kernels for 32% -> 23%
where the time goes in v4:
time: 93.2 us; the launch traced here: 92.8 us
  waiting for transfers between devices  38.2 us (41%)
  Pallas kernels  23.8 us (26%)
  starting transfers between devices  15.5 us (17%)
  blocking collectives  14.5 us (16%)
    ppermute x7, waiting for transfers between devices, body(): arrived = {m: lax.ppermute(sends[m], 'space', route(*m, 0)) for m in MOVES}  32.8 us
    all_to_all x1, blocking collectives, body(): lax.all_to_all(partial, 'space', split_axis=0, concat_axis=0, tiled=True)  14.5 us
    ppermute x7, starting transfers between devices, body(): arrived = {m: lax.ppermute(sends[m], 'space', route(*m, 0)) for m in MOVES}  14 us
    pallas_call x2, Pallas kernels, pack_vectors(): pl.pallas_call(kernel, grid=(times // 2,), in_specs=[pl.BlockSpec((1, row...  10.2 us
    pallas_call x4, Pallas kernels, pack_solutions(): pl.pallas_call(kernel, grid=(rows // block_rows,), in_specs=[source(m) fo...  8.47 us
    ppermute x1, waiting for transfers between devices, body(): swapped = lax.ppermute(raw, 'space', route(0, 0, 1))  5.38 us
    pallas_call x8, Pallas kernels, product(): pl.pallas_call(kernel, grid=(1,), in_specs=[vec_spec, vec_spec, pl.BlockS...  5.12 us
  transfers between devices with their start and end apart: 8, of which 4 were waited for; matrix products, arithmetic and copies ran while one was open for 0% of the time, Pallas kernels for 23%

profile of v4, /device:TPU:1, one launch (start us, length us, event | category | flops | bytes accessed | tf_op | source)
XLA Modules:
  0.0 92.8 jit_solution(2498043157466318228)
XLA Ops:
  0.0 1.5 %shard_map.28 = bf16[2,2,64,1536]{3,2,1,0:T(8,128)(2,1)S(1)} custom-call(bf16[1,64,3,16,8,128]{5,4,3,2,1,0:T(8,128)(2,1)} %bitcast.34), custom_call_target="tpu_custom_call" | custom-call | tf_op jit(solution)/shard_map/pallas_call | solution.py:61
  1.5 1.5 %collective-permute-start = (bf16[16,128,2,3,512]{4,2,3,1,0:T(2,128)(2,1)}, bf16[16,128,2,3,512]{4,2,3,1,0:T(2,128)(2,1)S(1)}, u32[]{:S(2)}, u32[]{:S(2)}) collective-permute-start(bf16[16,128,2,3,512]{4,2,3,1,0:T(2,128)(2,1)} %param.3), channel_id=1, source_target_pairs={{0,1},{1,0},{2,3},{3,2},{4,5},{5,4},{6,7},{7,6},{8,9},{9,8},{10,11... | collective-permute-start | bytes 37748744 | tf_op jit(solution)/shard_map/ppermute | solution.py:150
  3.0 3.9 %collective-permute-start.7 = (bf16[2,2,64,1536]{3,2,1,0:T(8,128)(2,1)S(1)}, bf16[2,2,64,1536]{3,2,1,0:T(8,128)(2,1)S(1)}, u32[]{:S(2)}, u32[]{:S(2)}) collective-permute-start(bf16[2,2,64,1536]{3,2,1,0:T(8,128)(2,1)S(1)} %shard_map.28), channel_id=1, source_target_pairs={{0,12},{1,13},{2,14},{3,15},{4,8},{5,9},{6,10},{7,11},{8,4},{9,5},... | collective-permute-start | bytes 2359304 | tf_op jit(solution)/shard_map/ppermute | solution.py:152
  7.0 2.1 %shard_map.29 = (bf16[2,2,64,1536]{3,2,1,0:T(8,128)(2,1)S(1)}, bf16[2,2,64,1536]{3,2,1,0:T(8,128)(2,1)S(1)}) custom-call(bf16[1,64,3,16,8,128]{5,4,3,2,1,0:T(8,128)(2,1)} %bitcast.35, bf16[1,64,3,16,8,128]{5,4,3,2,1,0:T(8,128)(2,1)} %bitcast.36), custom_call_target="tpu_custom_call" | custom-call | tf_op jit(solution)/shard_map/pallas_call | solution.py:61
  9.1 0.1 collective-permute-start.6
  9.2 0.3 collective-permute-start.5
  9.5 2.1 %shard_map.30 = (bf16[2,2,64,1536]{3,2,1,0:T(8,128)(2,1)S(1)}, bf16[2,2,64,1536]{3,2,1,0:T(8,128)(2,1)S(1)}) custom-call(bf16[1,64,3,16,8,128]{5,4,3,2,1,0:T(8,128)(2,1)} %bitcast.37, bf16[1,64,3,16,8,128]{5,4,3,2,1,0:T(8,128)(2,1)} %bitcast.38), custom_call_target="tpu_custom_call" | custom-call | tf_op jit(solution)/shard_map/pallas_call | solution.py:61
  11.6 2.3 %collective-permute-start.4 = (bf16[2,2,64,1536]{3,2,1,0:T(8,128)(2,1)S(1)}, bf16[2,2,64,1536]{3,2,1,0:T(8,128)(2,1)S(1)}, u32[]{:S(2)}, u32[]{:S(2)}) collective-permute-start(bf16[2,2,64,1536]{3,2,1,0:T(8,128)(2,1)S(1)} %get-tuple-element.31), channel_id=1, source_target_pairs={{0,10},{1,11},{2,12},{3,13},{4,14},{5,15},{6,8},{7,9},{8,2},{9,3},... | collective-permute-start | bytes 2359304 | tf_op jit(solution)/shard_map/ppermute | solution.py:152
  13.9 2.7 %shard_map.31 = (bf16[2,2,64,1536]{3,2,1,0:T(8,128)(2,1)S(1)}, bf16[2,2,64,1536]{3,2,1,0:T(8,128)(2,1)S(1)}, bf16[2,2,64,1536]{3,2,1,0:T(8,128)(2,1)S(1)}) custom-call(bf16[1,64,3,16,8,128]{5,4,3,2,1,0:T(8,128)(2,1)} %bitcast.39, bf16[1,64,3,16,8,128]{5,4,3,2,1,0:T(8,128)(2,1)} %bitcast.40, bf16[1,64,3,16,8,128]{5,4,3,2,1,0:T(8,128)(2,1)} %bitcast.41), custom_call_target="tpu_custom_call" | custom-call | tf_op jit(solution)/shard_map/pallas_call | solution.py:61
  16.6 5.4 %collective-permute-done = bf16[16,128,2,3,512]{4,2,3,1,0:T(2,128)(2,1)S(1)} collective-permute-done((bf16[16,128,2,3,512]{4,2,3,1,0:T(2,128)(2,1)}, bf16[16,128,2,3,512]{4,2,3,1,0:T(2,128)(2,1)S(1)}, u32[]{:S(2)}, u32[]{:S(2)}) %collective-permute-start) | collective-permute-done | bytes 12582944 | tf_op jit(solution)/shard_map/ppermute | solution.py:150
  22.0 2.8 %collective-permute-start.3 = (bf16[2,2,64,1536]{3,2,1,0:T(8,128)(2,1)S(1)}, bf16[2,2,64,1536]{3,2,1,0:T(8,128)(2,1)S(1)}, u32[]{:S(2)}, u32[]{:S(2)}) collective-permute-start(bf16[2,2,64,1536]{3,2,1,0:T(8,128)(2,1)S(1)} %get-tuple-element.30), channel_id=1, source_target_pairs={{0,6},{1,7},{2,0},{3,1},{4,2},{5,3},{6,4},{7,5},{8,14},{9,15},{10,... | collective-permute-start | bytes 2359304 | tf_op jit(solution)/shard_map/ppermute | solution.py:152
  24.8 0.0 collective-permute-done.7.sol
  24.8 3.5 %collective-permute-start.2 = (bf16[2,2,64,1536]{3,2,1,0:T(8,128)(2,1)S(1)}, bf16[2,2,64,1536]{3,2,1,0:T(8,128)(2,1)S(1)}, u32[]{:S(2)}, u32[]{:S(2)}) collective-permute-start(bf16[2,2,64,1536]{3,2,1,0:T(8,128)(2,1)S(1)} %get-tuple-element.29), channel_id=1, source_target_pairs={{0,14},{1,15},{2,8},{3,9},{4,10},{5,11},{6,12},{7,13},{8,6},{9,7},... | collective-permute-start | bytes 2359304 | tf_op jit(solution)/shard_map/ppermute | solution.py:152
  28.3 13.8 %collective-permute-done.6.sol = bf16[2,2,64,1536]{3,2,1,0:T(8,128)(2,1)S(1)} collective-permute-done((bf16[2,2,64,1536]{3,2,1,0:T(8,128)(2,1)S(1)}, bf16[2,2,64,1536]{3,2,1,0:T(8,128)(2,1)S(1)}, u32[]{:S(2)}, u32[]{:S(2)}) %collective-permute-start.6) | collective-permute-done | bytes 786464 | tf_op jit(solution)/shard_map/ppermute | solution.py:152
  42.1 1.1 %collective-permute-start.1 = (bf16[2,2,64,1536]{3,2,1,0:T(8,128)(2,1)S(1)}, bf16[2,2,64,1536]{3,2,1,0:T(8,128)(2,1)S(1)}, u32[]{:S(2)}, u32[]{:S(2)}) collective-permute-start(bf16[2,2,64,1536]{3,2,1,0:T(8,128)(2,1)S(1)} %get-tuple-element.28), channel_id=1, source_target_pairs={{0,2},{1,3},{2,4},{3,5},{4,6},{5,7},{6,0},{7,1},{8,10},{9,11},{10,... | collective-permute-start | bytes 2359304 | tf_op jit(solution)/shard_map/ppermute | solution.py:152
  43.2 6.8 %shard_map.32.near = bf16[8,2,128,1536]{3,2,1,0:T(8,128)(2,1)S(1)} custom-call(bf16[16,128,3,1,8,128]{5,4,3,2,1,0:T(8,128)(2,1)} %bitcast.42), custom_call_target="tpu_custom_call" | custom-call | tf_op jit(solution)/shard_map/pallas_call | solution.py:80
  50.1 3.4 %shard_map.33.far = bf16[8,2,128,1536]{3,2,1,0:T(8,128)(2,1)S(1)} custom-call(bf16[16,128,3,1,8,128]{5,4,3,2,1,0:T(8,128)(2,1)S(1)} %bitcast.33), custom_call_target="tpu_custom_call" | custom-call | tf_op jit(solution)/shard_map/pallas_call | solution.py:80
  53.5 0.6 shard_map.34.refs_0_
  54.1 0.6 shard_map.35.refs_0_
  54.7 0.6 shard_map.36.refs_0_
  55.4 0.0 collective-permute-done.5.sol
  55.4 0.6 shard_map.37.refs_0_
  56.0 3.1 %collective-permute-done.4.sol = bf16[2,2,64,1536]{3,2,1,0:T(8,128)(2,1)S(1)} collective-permute-done((bf16[2,2,64,1536]{3,2,1,0:T(8,128)(2,1)S(1)}, bf16[2,2,64,1536]{3,2,1,0:T(8,128)(2,1)S(1)}, u32[]{:S(2)}, u32[]{:S(2)}) %collective-permute-start.4) | collective-permute-done | bytes 786464 | tf_op jit(solution)/shard_map/ppermute | solution.py:152
  59.1 0.6 shard_map.38.refs_0_
  59.8 0.0 collective-permute-done.3.sol
  59.8 0.6 shard_map.39.refs_0_
  60.4 15.9 %collective-permute-done.2.sol = bf16[2,2,64,1536]{3,2,1,0:T(8,128)(2,1)S(1)} collective-permute-done((bf16[2,2,64,1536]{3,2,1,0:T(8,128)(2,1)S(1)}, bf16[2,2,64,1536]{3,2,1,0:T(8,128)(2,1)S(1)}, u32[]{:S(2)}, u32[]{:S(2)}) %collective-permute-start.2) | collective-permute-done | bytes 786464 | tf_op jit(solution)/shard_map/ppermute | solution.py:152
  76.3 0.6 shard_map.40.refs_0_
  77.0 0.0 collective-permute-done.1.sol
  77.0 0.6 shard_map.41
  77.6 14.5 %all_to_all.5 = f32[16,8,8,128]{3,2,1,0:T(8,128)S(1)} all-to-all(f32[16,8,8,128]{3,2,1,0:T(8,128)S(1)} %shard_map.41), channel_id=1, replica_groups=mesh['tm'=8,'space'=16] {'space'}, dimensions={0} | all-to-all | bytes 1048576 | tf_op jit(solution)/shard_map/all_to_all | solution.py:159
  92.2 0.6 copy.28
  (1 shorter events, 0.0 us)
Async XLA Ops:
  1.5 20.5 %collective-permute-start = (bf16[16,128,2,3,512]{4,2,3,1,0:T(2,128)(2,1)}, bf16[16,128,2,3,512]{4,2,3,1,0:T(2,128)(2,1)S(1)}, u32[]{:S(2)}, u32[]{:S(2)}) collective-permute-start(bf16[16,128,2,3,512]{4,2,3,1,0:T(2,128)(2,1)} %param.3), channel_id=1, source_target_pairs={{0,1},{1,0},{2,3},{3,2},{4,5},{5,4},{6,7},{7,6},{8,9},{9,8},{10,11... | collective-permute-start | bytes 37748744 | tf_op jit(solution)/shard_map/ppermute | solution.py:150
  3.0 21.8 %collective-permute-start.7 = (bf16[2,2,64,1536]{3,2,1,0:T(8,128)(2,1)S(1)}, bf16[2,2,64,1536]{3,2,1,0:T(8,128)(2,1)S(1)}, u32[]{:S(2)}, u32[]{:S(2)}) collective-permute-start(bf16[2,2,64,1536]{3,2,1,0:T(8,128)(2,1)S(1)} %shard_map.28), channel_id=1, source_target_pairs={{0,12},{1,13},{2,14},{3,15},{4,8},{5,9},{6,10},{7,11},{8,4},{9,5},... | collective-permute-start | bytes 2359304 | tf_op jit(solution)/shard_map/ppermute | solution.py:152
  9.1 33.0 %collective-permute-start.6 = (bf16[2,2,64,1536]{3,2,1,0:T(8,128)(2,1)S(1)}, bf16[2,2,64,1536]{3,2,1,0:T(8,128)(2,1)S(1)}, u32[]{:S(2)}, u32[]{:S(2)}) collective-permute-start(bf16[2,2,64,1536]{3,2,1,0:T(8,128)(2,1)S(1)} %get-tuple-element.32), channel_id=1, source_target_pairs={{0,4},{1,5},{2,6},{3,7},{4,0},{5,1},{6,2},{7,3},{8,12},{9,13},{10,... | collective-permute-start | bytes 2359304 | tf_op jit(solution)/shard_map/ppermute | solution.py:152
  9.2 46.2 %collective-permute-start.5 = (bf16[2,2,64,1536]{3,2,1,0:T(8,128)(2,1)S(1)}, bf16[2,2,64,1536]{3,2,1,0:T(8,128)(2,1)S(1)}, u32[]{:S(2)}, u32[]{:S(2)}) collective-permute-start(bf16[2,2,64,1536]{3,2,1,0:T(8,128)(2,1)S(1)} %get-tuple-element.20), channel_id=1, source_target_pairs={{0,8},{1,9},{2,10},{3,11},{4,12},{5,13},{6,14},{7,15},{8,0},{9,1},... | collective-permute-start | bytes 2359304 | tf_op jit(solution)/shard_map/ppermute | solution.py:152
  11.6 47.5 %collective-permute-start.4 = (bf16[2,2,64,1536]{3,2,1,0:T(8,128)(2,1)S(1)}, bf16[2,2,64,1536]{3,2,1,0:T(8,128)(2,1)S(1)}, u32[]{:S(2)}, u32[]{:S(2)}) collective-permute-start(bf16[2,2,64,1536]{3,2,1,0:T(8,128)(2,1)S(1)} %get-tuple-element.31), channel_id=1, source_target_pairs={{0,10},{1,11},{2,12},{3,13},{4,14},{5,15},{6,8},{7,9},{8,2},{9,3},... | collective-permute-start | bytes 2359304 | tf_op jit(solution)/shard_map/ppermute | solution.py:152
  22.0 37.7 %collective-permute-start.3 = (bf16[2,2,64,1536]{3,2,1,0:T(8,128)(2,1)S(1)}, bf16[2,2,64,1536]{3,2,1,0:T(8,128)(2,1)S(1)}, u32[]{:S(2)}, u32[]{:S(2)}) collective-permute-start(bf16[2,2,64,1536]{3,2,1,0:T(8,128)(2,1)S(1)} %get-tuple-element.30), channel_id=1, source_target_pairs={{0,6},{1,7},{2,0},{3,1},{4,2},{5,3},{6,4},{7,5},{8,14},{9,15},{10,... | collective-permute-start | bytes 2359304 | tf_op jit(solution)/shard_map/ppermute | solution.py:152
  24.8 51.5 %collective-permute-start.2 = (bf16[2,2,64,1536]{3,2,1,0:T(8,128)(2,1)S(1)}, bf16[2,2,64,1536]{3,2,1,0:T(8,128)(2,1)S(1)}, u32[]{:S(2)}, u32[]{:S(2)}) collective-permute-start(bf16[2,2,64,1536]{3,2,1,0:T(8,128)(2,1)S(1)} %get-tuple-element.29), channel_id=1, source_target_pairs={{0,14},{1,15},{2,8},{3,9},{4,10},{5,11},{6,12},{7,13},{8,6},{9,7},... | collective-permute-start | bytes 2359304 | tf_op jit(solution)/shard_map/ppermute | solution.py:152
  42.1 34.9 %collective-permute-start.1 = (bf16[2,2,64,1536]{3,2,1,0:T(8,128)(2,1)S(1)}, bf16[2,2,64,1536]{3,2,1,0:T(8,128)(2,1)S(1)}, u32[]{:S(2)}, u32[]{:S(2)}) collective-permute-start(bf16[2,2,64,1536]{3,2,1,0:T(8,128)(2,1)S(1)} %get-tuple-element.28), channel_id=1, source_target_pairs={{0,2},{1,3},{2,4},{3,5},{4,6},{5,7},{6,0},{7,1},{8,10},{9,11},{10,... | collective-permute-start | bytes 2359304 | tf_op jit(solution)/shard_map/ppermute | solution.py:152

commit v5 on v4

--- a/solution.py
+++ b/solution.py
@@ -9,8 +9,7 @@
 VMEM = 8 * 2**20
 FREE = pl.CostEstimate(flops=0, bytes_accessed=0, transcendentals=0)
 RING = 4
-MOVES = [(1, 2), (0, 2), (1, 0), (1, 1), (1, 3), (0, 3), (0, 1)]
-LAST = [(0, 3), (1, 3), (0, 1)]
+MOVES = [(1, 2), (0, 2), (1, 0), (1, 1), (0, 3), (1, 3), (0, 1)]
 
 
 def tile_view(a, groups):
@@ -127,6 +126,24 @@
     )(near, far, sol, *held)
 
 
+def add_up(partial):
+    chips, cores, times, rows, cols = partial.shape
+
+    def kernel(src, dst):
+        for c in range(cores):
+            total = src[0, c]
+            for n in range(1, chips):
+                total += src[n, c]
+            dst[:, c] = total
+
+    return pl.pallas_call(
+        kernel,
+        out_shape=jax.ShapeDtypeStruct((times, cores, rows, cols), partial.dtype),
+        compiler_params=pltpu.CompilerParams(vmem_limit_bytes=VMEM),
+        cost_estimate=FREE,
+    )(partial)
+
+
 def body(solutions, eigvecs):
     shares = lax.axis_size("space")
     chips = shares // 2
@@ -154,12 +171,11 @@
     near = pack_vectors(held_view(eigvecs, 1, done))
     far = pack_vectors(tile_view(swapped, 1))
     partial = None
-    for move in [(0, 0)] + MOVES[:4] + LAST:
+    for move in [(0, 0)] + MOVES:
         partial = product(near, far, arrived[move], move, partial, shares)
     partial = lax.all_to_all(partial, "space", split_axis=0, concat_axis=0, tiled=True)
     partial = partial.reshape(chips, 2, chips, -1, partial.shape[-1])
-    total = jnp.sum(partial, axis=0)
-    return jnp.swapaxes(total, 0, 1).reshape(shares, -1, total.shape[-1])
+    return add_up(partial).reshape(shares, -1, partial.shape[-1])
 
 
 def solution(mesh):

time: 93.2 us -> 93.2 us (level)
  no operation moved by 1% of the time
where the time goes in v5:
time: 93.2 us; the launch traced here: 92.8 us
  waiting for transfers between devices  38.2 us (41%)
  Pallas kernels  24.5 us (26%)
  starting transfers between devices  15.5 us (17%)
  blocking collectives  14.5 us (16%)
    ppermute x7, waiting for transfers between devices, body(): arrived = {m: lax.ppermute(sends[m], 'space', route(*m, 0)) for m in MOVES}  32.8 us
    all_to_all x1, blocking collectives, body(): lax.all_to_all(partial, 'space', split_axis=0, concat_axis=0, tiled=True)  14.5 us
    ppermute x7, starting transfers between devices, body(): arrived = {m: lax.ppermute(sends[m], 'space', route(*m, 0)) for m in MOVES}  14 us
    pallas_call x2, Pallas kernels, pack_vectors(): pl.pallas_call(kernel, grid=(times // 2,), in_specs=[pl.BlockSpec((1, row...  10.2 us
    pallas_call x4, Pallas kernels, pack_solutions(): pl.pallas_call(kernel, grid=(rows // block_rows,), in_specs=[source(m) fo...  8.47 us
    ppermute x1, waiting for transfers between devices, body(): swapped = lax.ppermute(raw, 'space', route(0, 0, 1))  5.38 us
    pallas_call x8, Pallas kernels, product(): pl.pallas_call(kernel, grid=(1,), in_specs=[vec_spec, vec_spec, pl.BlockS...  5.12 us
  transfers between devices with their start and end apart: 8, of which 4 were waited for; matrix products, arithmetic and copies ran while one was open for 0% of the time, Pallas kernels for 23%

profile of v5, /device:TPU:1, one launch (start us, length us, event | category | flops | bytes accessed | tf_op | source)
XLA Modules:
  0.0 92.8 jit_solution(2991893686876314953)
XLA Ops:
  0.0 1.5 %shard_map.28 = bf16[2,2,64,1536]{3,2,1,0:T(8,128)(2,1)S(1)} custom-call(bf16[1,64,3,16,8,128]{5,4,3,2,1,0:T(8,128)(2,1)} %bitcast.34), custom_call_target="tpu_custom_call" | custom-call | tf_op jit(solution)/shard_map/pallas_call | solution.py:60
  1.5 1.5 %collective-permute-start = (bf16[16,128,2,3,512]{4,2,3,1,0:T(2,128)(2,1)}, bf16[16,128,2,3,512]{4,2,3,1,0:T(2,128)(2,1)S(1)}, u32[]{:S(2)}, u32[]{:S(2)}) collective-permute-start(bf16[16,128,2,3,512]{4,2,3,1,0:T(2,128)(2,1)} %param.3), channel_id=1, source_target_pairs={{0,1},{1,0},{2,3},{3,2},{4,5},{5,4},{6,7},{7,6},{8,9},{9,8},{10,11... | collective-permute-start | bytes 37748744 | tf_op jit(solution)/shard_map/ppermute | solution.py:167
  3.0 3.9 %collective-permute-start.7 = (bf16[2,2,64,1536]{3,2,1,0:T(8,128)(2,1)S(1)}, bf16[2,2,64,1536]{3,2,1,0:T(8,128)(2,1)S(1)}, u32[]{:S(2)}, u32[]{:S(2)}) collective-permute-start(bf16[2,2,64,1536]{3,2,1,0:T(8,128)(2,1)S(1)} %shard_map.28), channel_id=1, source_target_pairs={{0,12},{1,13},{2,14},{3,15},{4,8},{5,9},{6,10},{7,11},{8,4},{9,5},... | collective-permute-start | bytes 2359304 | tf_op jit(solution)/shard_map/ppermute | solution.py:169
  7.0 2.1 %shard_map.29 = (bf16[2,2,64,1536]{3,2,1,0:T(8,128)(2,1)S(1)}, bf16[2,2,64,1536]{3,2,1,0:T(8,128)(2,1)S(1)}) custom-call(bf16[1,64,3,16,8,128]{5,4,3,2,1,0:T(8,128)(2,1)} %bitcast.35, bf16[1,64,3,16,8,128]{5,4,3,2,1,0:T(8,128)(2,1)} %bitcast.36), custom_call_target="tpu_custom_call" | custom-call | tf_op jit(solution)/shard_map/pallas_call | solution.py:60
  9.1 0.1 collective-permute-start.6
  9.2 0.3 collective-permute-start.5
  9.5 2.1 %shard_map.30 = (bf16[2,2,64,1536]{3,2,1,0:T(8,128)(2,1)S(1)}, bf16[2,2,64,1536]{3,2,1,0:T(8,128)(2,1)S(1)}) custom-call(bf16[1,64,3,16,8,128]{5,4,3,2,1,0:T(8,128)(2,1)} %bitcast.37, bf16[1,64,3,16,8,128]{5,4,3,2,1,0:T(8,128)(2,1)} %bitcast.38), custom_call_target="tpu_custom_call" | custom-call | tf_op jit(solution)/shard_map/pallas_call | solution.py:60
  11.6 2.3 %collective-permute-start.4 = (bf16[2,2,64,1536]{3,2,1,0:T(8,128)(2,1)S(1)}, bf16[2,2,64,1536]{3,2,1,0:T(8,128)(2,1)S(1)}, u32[]{:S(2)}, u32[]{:S(2)}) collective-permute-start(bf16[2,2,64,1536]{3,2,1,0:T(8,128)(2,1)S(1)} %get-tuple-element.31), channel_id=1, source_target_pairs={{0,10},{1,11},{2,12},{3,13},{4,14},{5,15},{6,8},{7,9},{8,2},{9,3},... | collective-permute-start | bytes 2359304 | tf_op jit(solution)/shard_map/ppermute | solution.py:169
  13.9 2.7 %shard_map.31 = (bf16[2,2,64,1536]{3,2,1,0:T(8,128)(2,1)S(1)}, bf16[2,2,64,1536]{3,2,1,0:T(8,128)(2,1)S(1)}, bf16[2,2,64,1536]{3,2,1,0:T(8,128)(2,1)S(1)}) custom-call(bf16[1,64,3,16,8,128]{5,4,3,2,1,0:T(8,128)(2,1)} %bitcast.39, bf16[1,64,3,16,8,128]{5,4,3,2,1,0:T(8,128)(2,1)} %bitcast.40, bf16[1,64,3,16,8,128]{5,4,3,2,1,0:T(8,128)(2,1)} %bitcast.41), custom_call_target="tpu_custom_call" | custom-call | tf_op jit(solution)/shard_map/pallas_call | solution.py:60
  16.6 5.4 %collective-permute-done = bf16[16,128,2,3,512]{4,2,3,1,0:T(2,128)(2,1)S(1)} collective-permute-done((bf16[16,128,2,3,512]{4,2,3,1,0:T(2,128)(2,1)}, bf16[16,128,2,3,512]{4,2,3,1,0:T(2,128)(2,1)S(1)}, u32[]{:S(2)}, u32[]{:S(2)}) %collective-permute-start) | collective-permute-done | bytes 12582944 | tf_op jit(solution)/shard_map/ppermute | solution.py:167
  22.0 2.8 %collective-permute-start.3 = (bf16[2,2,64,1536]{3,2,1,0:T(8,128)(2,1)S(1)}, bf16[2,2,64,1536]{3,2,1,0:T(8,128)(2,1)S(1)}, u32[]{:S(2)}, u32[]{:S(2)}) collective-permute-start(bf16[2,2,64,1536]{3,2,1,0:T(8,128)(2,1)S(1)} %get-tuple-element.30), channel_id=1, source_target_pairs={{0,6},{1,7},{2,0},{3,1},{4,2},{5,3},{6,4},{7,5},{8,14},{9,15},{10,... | collective-permute-start | bytes 2359304 | tf_op jit(solution)/shard_map/ppermute | solution.py:169
  24.8 0.0 collective-permute-done.7.sol
  24.8 3.5 %collective-permute-start.2 = (bf16[2,2,64,1536]{3,2,1,0:T(8,128)(2,1)S(1)}, bf16[2,2,64,1536]{3,2,1,0:T(8,128)(2,1)S(1)}, u32[]{:S(2)}, u32[]{:S(2)}) collective-permute-start(bf16[2,2,64,1536]{3,2,1,0:T(8,128)(2,1)S(1)} %get-tuple-element.29), channel_id=1, source_target_pairs={{0,14},{1,15},{2,8},{3,9},{4,10},{5,11},{6,12},{7,13},{8,6},{9,7},... | collective-permute-start | bytes 2359304 | tf_op jit(solution)/shard_map/ppermute | solution.py:169
  28.3 13.8 %collective-permute-done.6.sol = bf16[2,2,64,1536]{3,2,1,0:T(8,128)(2,1)S(1)} collective-permute-done((bf16[2,2,64,1536]{3,2,1,0:T(8,128)(2,1)S(1)}, bf16[2,2,64,1536]{3,2,1,0:T(8,128)(2,1)S(1)}, u32[]{:S(2)}, u32[]{:S(2)}) %collective-permute-start.6) | collective-permute-done | bytes 786464 | tf_op jit(solution)/shard_map/ppermute | solution.py:169
  42.1 1.1 %collective-permute-start.1 = (bf16[2,2,64,1536]{3,2,1,0:T(8,128)(2,1)S(1)}, bf16[2,2,64,1536]{3,2,1,0:T(8,128)(2,1)S(1)}, u32[]{:S(2)}, u32[]{:S(2)}) collective-permute-start(bf16[2,2,64,1536]{3,2,1,0:T(8,128)(2,1)S(1)} %get-tuple-element.28), channel_id=1, source_target_pairs={{0,2},{1,3},{2,4},{3,5},{4,6},{5,7},{6,0},{7,1},{8,10},{9,11},{10,... | collective-permute-start | bytes 2359304 | tf_op jit(solution)/shard_map/ppermute | solution.py:169
  43.2 6.8 %shard_map.32.near = bf16[8,2,128,1536]{3,2,1,0:T(8,128)(2,1)S(1)} custom-call(bf16[16,128,3,1,8,128]{5,4,3,2,1,0:T(8,128)(2,1)} %bitcast.42), custom_call_target="tpu_custom_call" | custom-call | tf_op jit(solution)/shard_map/pallas_call | solution.py:79
  50.1 3.4 %shard_map.33.far = bf16[8,2,128,1536]{3,2,1,0:T(8,128)(2,1)S(1)} custom-call(bf16[16,128,3,1,8,128]{5,4,3,2,1,0:T(8,128)(2,1)S(1)} %bitcast.32), custom_call_target="tpu_custom_call" | custom-call | tf_op jit(solution)/shard_map/pallas_call | solution.py:79
  53.5 0.6 shard_map.34.refs_0_
  54.1 0.6 shard_map.35.refs_0_
  54.7 0.6 shard_map.36.refs_0_
  55.4 0.0 collective-permute-done.5.sol
  55.4 0.6 shard_map.37.refs_0_
  56.0 3.1 %collective-permute-done.4.sol = bf16[2,2,64,1536]{3,2,1,0:T(8,128)(2,1)S(1)} collective-permute-done((bf16[2,2,64,1536]{3,2,1,0:T(8,128)(2,1)S(1)}, bf16[2,2,64,1536]{3,2,1,0:T(8,128)(2,1)S(1)}, u32[]{:S(2)}, u32[]{:S(2)}) %collective-permute-start.4) | collective-permute-done | bytes 786464 | tf_op jit(solution)/shard_map/ppermute | solution.py:169
  59.1 0.6 shard_map.38.refs_0_
  59.8 0.0 collective-permute-done.3.sol
  59.8 0.6 shard_map.39.refs_0_
  60.4 15.9 %collective-permute-done.2.sol = bf16[2,2,64,1536]{3,2,1,0:T(8,128)(2,1)S(1)} collective-permute-done((bf16[2,2,64,1536]{3,2,1,0:T(8,128)(2,1)S(1)}, bf16[2,2,64,1536]{3,2,1,0:T(8,128)(2,1)S(1)}, u32[]{:S(2)}, u32[]{:S(2)}) %collective-permute-start.2) | collective-permute-done | bytes 786464 | tf_op jit(solution)/shard_map/ppermute | solution.py:169
  76.3 0.6 shard_map.40.refs_0_
  77.0 0.0 collective-permute-done.1.sol
  77.0 0.6 shard_map.41
  77.6 14.5 %all_to_all.5 = f32[16,8,8,128]{3,2,1,0:T(8,128)S(1)} all-to-all(f32[16,8,8,128]{3,2,1,0:T(8,128)S(1)} %shard_map.41), channel_id=1, replica_groups=mesh['tm'=8,'space'=16] {'space'}, dimensions={0} | all-to-all | bytes 1048576 | tf_op jit(solution)/shard_map/all_to_all | solution.py:176
  92.2 0.7 shard_map.42
Async XLA Ops:
  1.5 20.5 %collective-permute-start = (bf16[16,128,2,3,512]{4,2,3,1,0:T(2,128)(2,1)}, bf16[16,128,2,3,512]{4,2,3,1,0:T(2,128)(2,1)S(1)}, u32[]{:S(2)}, u32[]{:S(2)}) collective-permute-start(bf16[16,128,2,3,512]{4,2,3,1,0:T(2,128)(2,1)} %param.3), channel_id=1, source_target_pairs={{0,1},{1,0},{2,3},{3,2},{4,5},{5,4},{6,7},{7,6},{8,9},{9,8},{10,11... | collective-permute-start | bytes 37748744 | tf_op jit(solution)/shard_map/ppermute | solution.py:167
  3.0 21.8 %collective-permute-start.7 = (bf16[2,2,64,1536]{3,2,1,0:T(8,128)(2,1)S(1)}, bf16[2,2,64,1536]{3,2,1,0:T(8,128)(2,1)S(1)}, u32[]{:S(2)}, u32[]{:S(2)}) collective-permute-start(bf16[2,2,64,1536]{3,2,1,0:T(8,128)(2,1)S(1)} %shard_map.28), channel_id=1, source_target_pairs={{0,12},{1,13},{2,14},{3,15},{4,8},{5,9},{6,10},{7,11},{8,4},{9,5},... | collective-permute-start | bytes 2359304 | tf_op jit(solution)/shard_map/ppermute | solution.py:169
  9.1 33.0 %collective-permute-start.6 = (bf16[2,2,64,1536]{3,2,1,0:T(8,128)(2,1)S(1)}, bf16[2,2,64,1536]{3,2,1,0:T(8,128)(2,1)S(1)}, u32[]{:S(2)}, u32[]{:S(2)}) collective-permute-start(bf16[2,2,64,1536]{3,2,1,0:T(8,128)(2,1)S(1)} %get-tuple-element.32), channel_id=1, source_target_pairs={{0,4},{1,5},{2,6},{3,7},{4,0},{5,1},{6,2},{7,3},{8,12},{9,13},{10,... | collective-permute-start | bytes 2359304 | tf_op jit(solution)/shard_map/ppermute | solution.py:169
  9.2 46.2 %collective-permute-start.5 = (bf16[2,2,64,1536]{3,2,1,0:T(8,128)(2,1)S(1)}, bf16[2,2,64,1536]{3,2,1,0:T(8,128)(2,1)S(1)}, u32[]{:S(2)}, u32[]{:S(2)}) collective-permute-start(bf16[2,2,64,1536]{3,2,1,0:T(8,128)(2,1)S(1)} %get-tuple-element.20), channel_id=1, source_target_pairs={{0,8},{1,9},{2,10},{3,11},{4,12},{5,13},{6,14},{7,15},{8,0},{9,1},... | collective-permute-start | bytes 2359304 | tf_op jit(solution)/shard_map/ppermute | solution.py:169
  11.6 47.5 %collective-permute-start.4 = (bf16[2,2,64,1536]{3,2,1,0:T(8,128)(2,1)S(1)}, bf16[2,2,64,1536]{3,2,1,0:T(8,128)(2,1)S(1)}, u32[]{:S(2)}, u32[]{:S(2)}) collective-permute-start(bf16[2,2,64,1536]{3,2,1,0:T(8,128)(2,1)S(1)} %get-tuple-element.31), channel_id=1, source_target_pairs={{0,10},{1,11},{2,12},{3,13},{4,14},{5,15},{6,8},{7,9},{8,2},{9,3},... | collective-permute-start | bytes 2359304 | tf_op jit(solution)/shard_map/ppermute | solution.py:169
  22.0 37.7 %collective-permute-start.3 = (bf16[2,2,64,1536]{3,2,1,0:T(8,128)(2,1)S(1)}, bf16[2,2,64,1536]{3,2,1,0:T(8,128)(2,1)S(1)}, u32[]{:S(2)}, u32[]{:S(2)}) collective-permute-start(bf16[2,2,64,1536]{3,2,1,0:T(8,128)(2,1)S(1)} %get-tuple-element.30), channel_id=1, source_target_pairs={{0,6},{1,7},{2,0},{3,1},{4,2},{5,3},{6,4},{7,5},{8,14},{9,15},{10,... | collective-permute-start | bytes 2359304 | tf_op jit(solution)/shard_map/ppermute | solution.py:169
  24.8 51.5 %collective-permute-start.2 = (bf16[2,2,64,1536]{3,2,1,0:T(8,128)(2,1)S(1)}, bf16[2,2,64,1536]{3,2,1,0:T(8,128)(2,1)S(1)}, u32[]{:S(2)}, u32[]{:S(2)}) collective-permute-start(bf16[2,2,64,1536]{3,2,1,0:T(8,128)(2,1)S(1)} %get-tuple-element.29), channel_id=1, source_target_pairs={{0,14},{1,15},{2,8},{3,9},{4,10},{5,11},{6,12},{7,13},{8,6},{9,7},... | collective-permute-start | bytes 2359304 | tf_op jit(solution)/shard_map/ppermute | solution.py:169
  42.1 34.9 %collective-permute-start.1 = (bf16[2,2,64,1536]{3,2,1,0:T(8,128)(2,1)S(1)}, bf16[2,2,64,1536]{3,2,1,0:T(8,128)(2,1)S(1)}, u32[]{:S(2)}, u32[]{:S(2)}) collective-permute-start(bf16[2,2,64,1536]{3,2,1,0:T(8,128)(2,1)S(1)} %get-tuple-element.28), channel_id=1, source_target_pairs={{0,2},{1,3},{2,4},{3,5},{4,6},{5,7},{6,0},{7,1},{8,10},{9,11},{10,... | collective-permute-start | bytes 2359304 | tf_op jit(solution)/shard_map/ppermute | solution.py:169
